TPU v7x, 256 devices: a whole 4x4x8 slice. The times are simulated.
256 devices in a mesh: dp: 32 (over z, y_lo, core), hst: 8 (over y_hi, x).
Axes of the slice: x: 4, y: 4 (y_hi: 2, y_lo: 2; y = y_hi * 2 + y_lo), z: 8, core: 2. Of those that a mesh axis runs over, the one named last changes fastest.
Arguments:
- picture_features: bfloat16 [65536, 1152], P(('dp', 'hst')), may hold values from -6 to 6
- caption_features: bfloat16 [65536, 1152], P(('dp', 'hst')), may hold values from -6 to 6
- matching_caption_slot: int32 [32, 2048], P('dp'), may hold values from 0 to 2047, each once within a row
- score_inverse_heat: float32 [1], replicated, may hold values from 8 to 24
- score_offset: float32 [1], replicated, may hold values from -2 to 0.5
Outputs:
- row_loss: float32 [65536], P(('dp', 'hst'))
- grad_image: bfloat16 [65536, 1152], P(('dp', 'hst'))
- grad_text: bfloat16 [65536, 1152], P(('dp', 'hst'))
Inputs may be any that keep to these rules, and one draw needn't show every extreme that they name: Each row of matching_caption_slot holds every number of 0 to 2047 once.
All inputs are finite; a program needn't handle non-finite values.
Results may differ from a plain program's by a relative error of at most 0.0051.
Values may be sent and summed in bfloat16 or wider, within the bound.
No kernel may reach another device: no remote copies, remote signals or barrier semaphores. Data moves between devices by JAX's collectives and lax.ppermute only.
A program may use at most 128 MiB of HBM per device.

v0:
```python
import jax
import jax.numpy as jnp
from jax import lax
from jax.sharding import PartitionSpec as P

FEATURE_DIM = 1152


def passed_along(value, axis, steps):
    count = lax.axis_size(axis)
    pairs = [(source, (source + steps) % count) for source in range(count)]
    return lax.ppermute(value, axis, pairs)


def pair_logits(image_rows, text_block, score_scaling_factor, offset):
    product = lax.dot_general(
        image_rows, text_block, (((1,), (1,)), ((), ())), preferred_element_type=jnp.float32
    )
    return score_scaling_factor * product + offset


def image_terms(image_rows, text_block, score_scaling_factor, offset, positive):
    logits = pair_logits(image_rows, text_block, score_scaling_factor, offset)
    labels = 2.0 * positive - 1.0
    pair_loss = jnp.sum(jax.nn.log_sigmoid(labels * logits), axis=1)
    coefficient = (score_scaling_factor * (jax.nn.sigmoid(logits) - positive)).astype(jnp.bfloat16)
    image_part = jnp.dot(coefficient, text_block, preferred_element_type=jnp.float32)
    return (pair_loss, image_part, coefficient)


def text_terms(coefficient, image_rows):
    return lax.dot_general(
        coefficient, image_rows, (((0,), (0,)), ((), ())), preferred_element_type=jnp.float32
    )


def on_device(
    picture_features, caption_features, matching_caption_slot, score_inverse_heat, score_offset
):
    local_rows = picture_features.shape[0]
    score_scaling_factor = score_inverse_heat[0] / FEATURE_DIM
    offset = score_offset[0]
    own_block = lax.all_gather(caption_features, "hst", axis=0, tiled=True)
    group_size = own_block.shape[0]
    lower_block = passed_along(own_block, "dp", 1)
    upper_block = passed_along(own_block, "dp", -1)
    first_row = lax.axis_index("hst") * local_rows
    targets = lax.dynamic_slice_in_dim(matching_caption_slot[0], first_row, local_rows)
    columns = jnp.arange(group_size, dtype=jnp.int32)
    positive = (columns[None, :] == targets[:, None]).astype(jnp.float32)
    nothing = jnp.zeros_like(positive)
    own_loss, own_image, own_coef = image_terms(
        picture_features, own_block, score_scaling_factor, offset, positive
    )
    low_loss, low_image, low_coef = image_terms(
        picture_features, lower_block, score_scaling_factor, offset, nothing
    )
    up_loss, up_image, up_coef = image_terms(
        picture_features, upper_block, score_scaling_factor, offset, nothing
    )
    row_loss = -(own_loss + low_loss + up_loss) / (3 * group_size)
    grad_image = (own_image + low_image + up_image).astype(jnp.bfloat16)
    own_text = text_terms(own_coef, picture_features)
    low_text = text_terms(low_coef, picture_features)
    up_text = text_terms(up_coef, picture_features)
    own_sum, low_sum, up_sum = (
        lax.psum_scatter(own_text, "hst", scatter_dimension=0, tiled=True),
        lax.psum_scatter(low_text, "hst", scatter_dimension=0, tiled=True),
        lax.psum_scatter(up_text, "hst", scatter_dimension=0, tiled=True),
    )
    from_below = passed_along(up_sum, "dp", 1)
    from_above = passed_along(low_sum, "dp", -1)
    summed_text = own_sum + from_below + from_above
    grad_text = summed_text.astype(jnp.bfloat16)
    return (row_loss, grad_image, grad_text)


def solution(mesh):
    in_specs = (P(("dp", "hst"), None), P(("dp", "hst"), None), P("dp", None), P(), P())
    out_specs = (P(("dp", "hst")), P(("dp", "hst"), None), P(("dp", "hst"), None))
    return jax.shard_map(
        on_device, mesh=mesh, in_specs=in_specs, out_specs=out_specs, check_vma=False
    )
```

profile of v0, /device:TPU:1, one launch (start us, length us, event | category | flops | bytes accessed | tf_op | source)
XLA Modules:
  0.0 601.3 jit_solution(5552642111792256936)
XLA Ops:
  7.2 0.0 copy-start
  7.2 0.0 all-gather.2.cloned.1.call-start
  7.2 0.7 all-gather.2.cloned.1.call-update
  7.9 0.0 reduce-scatter.6.cloned.1.call-start
  8.0 87.1 %all-gather.2.cloned.1.call-done = bf16[2048,1152]{1,0:T(8,128)(2,1)} async-done(((bf16[256,1152]{1,0:T(8,128)(2,1)}), bf16[2048,1152]{1,0:T(8,128)(2,1)}) %all-gather.2.cloned.1.call-update) | async-done | bytes 4718608 | tf_op jit(solution)/shard_map/all_gather | solution.py:43
  95.1 1.1 collective-permute-start.1
  97.4 51.4 %collective-permute-done.1 = bf16[2048,1152]{1,0:T(8,128)(2,1)S(1)} collective-permute-done((bf16[2048,1152]{1,0:T(8,128)(2,1)}, bf16[2048,1152]{1,0:T(8,128)(2,1)S(1)}, u32[]{:S(2)}, u32[]{:S(2)}) %collective-permute-start.1) | collective-permute-done | bytes 4718624 | tf_op jit(solution)/shard_map/ppermute | solution.py:12
  148.8 0.0 copy-start.1
  148.8 0.0 copy-done
  148.8 2.4 fusion.6
  151.3 0.0 copy-done.1
  151.3 0.0 copy-start.3
  151.3 1.4 copy-done.3
  152.6 5.5 fusion.8
  158.1 0.0 reduce-scatter.6.cloned.1.call-update
  158.2 0.0 reduce-scatter.8.cloned.1.call-start
  158.2 0.1 collective-permute-start
  158.3 89.3 %collective-permute-done = bf16[2048,1152]{1,0:T(8,128)(2,1)S(1)} collective-permute-done((bf16[2048,1152]{1,0:T(8,128)(2,1)}, bf16[2048,1152]{1,0:T(8,128)(2,1)S(1)}, u32[]{:S(2)}, u32[]{:S(2)}) %collective-permute-start) | collective-permute-done | bytes 4718624 | tf_op jit(solution)/shard_map/ppermute | solution.py:12
  247.6 0.0 copy-start.2
  247.6 2.4 fusion.5
  250.0 0.0 copy-done.2
  250.0 0.0 copy-start.5
  250.0 1.3 copy-done.5
  251.4 5.6 fusion.7
  257.0 0.0 reduce-scatter.8.cloned.1.call-update
  257.0 0.2 reduce-scatter.4.cloned.1.call-start
  257.2 0.7 constant_dynamic-slice_fusion
  257.9 5.3 fusion.4
  263.2 5.6 fusion.9
  268.8 0.0 reduce-scatter.4.cloned.1.call-update
  268.8 5.0 fusion.10
  273.9 53.3 %reduce-scatter.6.cloned.1.call-done = f32[256,1152]{1,0:T(8,128)} async-done(((f32[2048,1152]{1,0:T(8,128)}), f32[256,1152]{1,0:T(8,128)}) %reduce-scatter.6.cloned.1.call-update) | async-done | bytes 1179664 | tf_op jit(solution)/shard_map/reduce_scatter | solution.py:69
  327.2 1.3 collective-permute-start.2
  328.5 131.8 %reduce-scatter.8.cloned.1.call-done = f32[256,1152]{1,0:T(8,128)} async-done(((f32[2048,1152]{1,0:T(8,128)}), f32[256,1152]{1,0:T(8,128)}) %reduce-scatter.8.cloned.1.call-update) | async-done | bytes 1179664 | tf_op jit(solution)/shard_map/reduce_scatter | solution.py:68
  460.3 0.0 copy-start.4
  460.3 1.1 collective-permute-start.3
  461.5 4.8 convolution_add_fusion.1
  466.3 0.6 negate_multiply_fusion
  466.9 0.0 copy-done.4
  466.9 4.8 fusion.3
  471.6 120.9 %reduce-scatter.4.cloned.1.call-done = f32[256,1152]{1,0:T(8,128)} async-done(((f32[2048,1152]{1,0:T(8,128)}), f32[256,1152]{1,0:T(8,128)}) %reduce-scatter.4.cloned.1.call-update) | async-done | bytes 1179664 | tf_op jit(solution)/shard_map/reduce_scatter | solution.py:67
  592.5 0.0 collective-permute-done.2
  592.5 0.0 collective-permute-done.3
  592.5 2.3 add_convert_fusion
Async XLA Ops:
  7.2 141.7 %copy-start = (bf16[256,1152]{1,0:T(8,128)(2,1)S(1)}, bf16[256,1152]{1,0:T(8,128)(2,1)}, u32[]{:S(2)}) copy-start(bf16[256,1152]{1,0:T(8,128)(2,1)} %param.5) | copy-start | bytes 1769476
  7.2 87.9 %all-gather.2.cloned.1.call-start = ((), (), s32[]{:S(2)}) async-start(), calls=%async_computation.3 | async-start | bytes 5308416 | tf_op jit(solution)/shard_map/all_gather | solution.py:43
  7.9 319.3 %reduce-scatter.6.cloned.1.call-start = ((), (), s32[]{:S(2)}) async-start(), calls=%async_computation.5 | async-start | bytes 10616832 | tf_op jit(solution)/shard_map/reduce_scatter | solution.py:69
  95.1 53.8 %collective-permute-start.1 = (bf16[2048,1152]{1,0:T(8,128)(2,1)}, bf16[2048,1152]{1,0:T(8,128)(2,1)S(1)}, u32[]{:S(2)}, u32[]{:S(2)}) collective-permute-start(bf16[2048,1152]{1,0:T(8,128)(2,1)} %all-gather.2.cloned.1.call-done), channel_id=1, source_target_pairs={{0,248},{8,0},{16,8},{24,16},{32,24},{40,32},{48,40},{56,48},{64,5... | collective-permute-start | bytes 14155784 | tf_op jit(solution)/shard_map/ppermute | solution.py:12
  148.8 2.4 copy-start.1
  151.3 1.4 copy-start.3
  158.2 302.1 %reduce-scatter.8.cloned.1.call-start = ((), (), s32[]{:S(2)}) async-start(), calls=%async_computation.6 | async-start | bytes 10616832 | tf_op jit(solution)/shard_map/reduce_scatter | solution.py:68
  158.2 89.4 %collective-permute-start = (bf16[2048,1152]{1,0:T(8,128)(2,1)}, bf16[2048,1152]{1,0:T(8,128)(2,1)S(1)}, u32[]{:S(2)}, u32[]{:S(2)}) collective-permute-start(bf16[2048,1152]{1,0:T(8,128)(2,1)} %all-gather.2.cloned.1.call-done), channel_id=1, source_target_pairs={{0,8},{8,16},{16,24},{24,32},{32,40},{40,48},{48,56},{56,64},{64,7... | collective-permute-start | bytes 14155784 | tf_op jit(solution)/shard_map/ppermute | solution.py:12
  247.6 2.4 copy-start.2
  250.0 1.4 copy-start.5
  257.0 335.5 %reduce-scatter.4.cloned.1.call-start = ((), (), s32[]{:S(2)}) async-start(), calls=%async_computation.4 | async-start | bytes 10616832 | tf_op jit(solution)/shard_map/reduce_scatter | solution.py:67
  327.2 265.3 %collective-permute-start.2 = (f32[256,1152]{1,0:T(8,128)}, f32[256,1152]{1,0:T(8,128)S(1)}, u32[]{:S(2)}, u32[]{:S(2)}) collective-permute-start(f32[256,1152]{1,0:T(8,128)} %reduce-scatter.6.cloned.1.call-done), channel_id=1, source_target_pairs={{0,8},{8,16},{16,24},{24,32},{32,40},{40,48},{48,56},{56,64},{64,7... | collective-permute-start | bytes 3538952 | tf_op jit(solution)/shard_map/ppermute | solution.py:12
  460.3 6.6 %copy-start.4 = (f32[256,2048]{1,0:T(8,128)S(1)}, f32[256,2048]{1,0:T(8,128)}, u32[]{:S(2)}) copy-start(f32[256,2048]{1,0:T(8,128)} %copy-done.3) | copy-start | bytes 6291460
  460.3 132.2 %collective-permute-start.3 = (f32[256,1152]{1,0:T(8,128)}, f32[256,1152]{1,0:T(8,128)S(1)}, u32[]{:S(2)}, u32[]{:S(2)}) collective-permute-start(f32[256,1152]{1,0:T(8,128)} %reduce-scatter.8.cloned.1.call-done), channel_id=1, source_target_pairs={{0,248},{8,0},{16,8},{24,16},{32,24},{40,32},{48,40},{56,48},{64,5... | collective-permute-start | bytes 3538952 | tf_op jit(solution)/shard_map/ppermute | solution.py:12
Sparse Core Ops, SparseCore 0:
  10.6 84.3 all-gather.1
  158.3 168.8 reduce-scatter.5
  332.0 128.2 reduce-scatter.7
  464.4 128.0 reduce-scatter.3
where the time goes:
time: 602 us; the launch traced here: 601 us
  waiting for transfers between devices  534 us (89%)
  matrix products  41.5 us (7%)
  between operations  15.1 us (3%)
    ppermute x4, waiting for transfers between devices, passed_along(): return lax.ppermute(value, axis, pairs)  141 us
    reduce_scatter x1, waiting for transfers between devices, on_device(): lax.psum_scatter(low_text, 'hst', scatter_dimension=0, tiled=True)  132 us
    reduce_scatter x1, waiting for transfers between devices, on_device(): lax.psum_scatter(own_text, 'hst', scatter_dimension=0, tiled=True)  121 us
    all_gather x1, waiting for transfers between devices, on_device(): own_block = lax.all_gather(caption_features, 'hst', axis=0, tiled=True)  87.1 us
    reduce_scatter x1, waiting for transfers between devices, on_device(): lax.psum_scatter(up_text, 'hst', scatter_dimension=0, tiled=True)  53.3 us
    dot_general x3, matrix products, text_terms(): lax.dot_general(coefficient, image_rows, (((0,), (0,)), ((), ())), prefer...  16.7 us
    dot_general x3, matrix products, image_terms(): jnp.dot(coefficient, text_block, preferred_element_type=jnp.float32)  14.6 us
  transfers between devices with their start and end apart: 8, of which 6 were waited for; matrix products, arithmetic and copies ran while one was open for 6% of the time, Pallas kernels for 0%

commit v1 on v0

v1 whole, which is shorter than its diff:
```python
import functools

import jax
import jax.numpy as jnp
from jax import lax
from jax.experimental import pallas as pl
from jax.experimental.pallas import tpu as pltpu
from jax.sharding import PartitionSpec as P

FEATURE_DIM = 1152
ROWS = 256
LOG2E = 1.4426950408889634
LN2 = 0.6931471805599453
NT = (((1,), (1,)), ((), ()))
TN = (((0,), (0,)), ((), ()))
AXES = ("dp", "hst")
F32 = jnp.float32
BF16 = jnp.bfloat16


def place_of(index):
    dp, hst = divmod(index, 8)
    return hst % 4, (hst // 4) * 2 + (dp // 2) % 2, dp // 4, dp % 2


def index_of(x, y, z, core):
    x, y, z = x % 4, y % 4, z % 8
    return (z * 4 + (y % 2) * 2 + core) * 8 + (y // 2) * 4 + x


def x_step(steps, x, y, z, core):
    return x + steps, y, z, core


def q_step(steps, x, y, z, core):
    if y % 2 == 0:
        z = z - 1 if core == 0 else z
    else:
        z = z if core == 0 else z + 1
    return x, y + steps, z, 1 - core


def core_step(x, y, z, core):
    return x, y, z, 1 - core


def moved(value, step):
    pairs = [(i, index_of(*step(*place_of(i)))) for i in range(256)]
    return lax.ppermute(value, AXES, pairs)


def ring_gather(own, step):
    half = ROWS // 2
    before = moved(own, functools.partial(step, 1))
    after = moved(own, functools.partial(step, -1))
    far_a = moved(before[:half], functools.partial(step, 1))
    far_b = moved(after[half:], functools.partial(step, -1))
    return before, after, far_a, far_b


def ring_scatter(own, before, after, far, step):
    half = ROWS // 2
    got_a = moved(far[:half], functools.partial(step, 1))
    got_b = moved(far[half:], functools.partial(step, -1))
    after = jnp.concatenate([summed(after[:half], got_a), after[half:]])
    before = jnp.concatenate([before[:half], summed(before[half:], got_b)])
    from_before = moved(after, functools.partial(step, 1))
    from_after = moved(before, functools.partial(step, -1))
    return summed(own, from_before, from_after)


def summed(*terms):
    total = terms[0].astype(F32)
    for term in terms[1:]:
        total = total + term.astype(F32)
    return total.astype(BF16)


def pair_terms(product, factors, positive):
    z = product * factors[0] + factors[1]
    if positive is not None:
        z = jnp.where(positive, -z, z)
    e = jnp.exp2(-jnp.abs(z))
    u = 1.0 + e
    log_u = jnp.where(e < 2.0**-8, LOG2E * e * (1.0 - 0.5 * e), jnp.log2(u))
    softplus = jnp.maximum(z, 0.0) + log_u
    scale = factors[2]
    coefficient = jnp.where(z >= 0.0, scale, scale * e) * pltpu.reciprocal(u, approx=True)
    if positive is not None:
        coefficient = jnp.where(positive, -coefficient, coefficient)
    return coefficient, softplus


def tile_kernel(factors_ref, slot_ref, *refs):
    n_in = 4 + 8
    ins, outs = refs[:n_in], refs[n_in:]
    grad_image, grad_text, loss, images, texts, coef, sems = outs
    spots = [(ins[0], images.at[pl.ds(0, 256)]), (ins[1], images.at[pl.ds(256, 256)]),
             (ins[2], images.at[pl.ds(512, 256)]), (ins[3], images.at[pl.ds(768, 128)]),
             (ins[4], images.at[pl.ds(896, 128)]), (ins[5], texts.at[pl.ds(0, 256)]),
             (ins[6], texts.at[pl.ds(256, 256)]), (ins[7], texts.at[pl.ds(512, 256)]),
             (ins[8], texts.at[pl.ds(768, 128)]), (ins[9], texts.at[pl.ds(896, 128)]),
             (ins[10], texts.at[pl.ds(1024, 256)]), (ins[11], texts.at[pl.ds(1280, 256)])]
    copies = [pltpu.make_async_copy(a, b, sems.at[n]) for n, (a, b) in enumerate(spots)]
    for copy in copies:
        copy.start()
    factors = [factors_ref[n] for n in range(3)]
    columns = lax.broadcasted_iota(jnp.int32, (ROWS, ROWS), 1)
    needed = [(5,), (6,), (7,), (8, 9), (10,), (11,)]
    for n in range(5):
        copies[n].wait()
    sums = [None] * 4
    for t in range(6):
        for n in needed[t]:
            copies[n].wait()
        text = texts[pl.ds(t * ROWS, ROWS), :]
        for i in range(4):
            image = images[pl.ds(i * ROWS, ROWS), :]
            product = lax.dot_general(image, text, NT, preferred_element_type=F32)
            positive = None
            if t in (0, 3):
                place = slot_ref[pl.ds(i * ROWS, ROWS), pl.ds(t // 3, 1)]
                positive = columns == place
            coefficient, softplus = pair_terms(product, factors, positive)
            coef[pl.ds(i * ROWS, ROWS), pl.ds(t * ROWS, ROWS)] = coefficient.astype(BF16)
            part = softplus[:, :128] + softplus[:, 128:]
            sums[i] = part if sums[i] is None else sums[i] + part
        grad_text[pl.ds(t * ROWS, ROWS), :] = lax.dot_general(
            coef[:, pl.ds(t * ROWS, ROWS)], images[...], TN, preferred_element_type=F32
        ).astype(BF16)
    for i in range(4):
        loss[pl.ds(i, 1), :] = jnp.sum(sums[i].T, axis=0, keepdims=True)
        grad_image[pl.ds(i * ROWS, ROWS), :] = jnp.dot(
            coef[pl.ds(i * ROWS, ROWS), :], texts[...], preferred_element_type=F32
        ).astype(BF16)


def tile(factors, slots, *blocks):
    any_spec = pl.BlockSpec(memory_space=pl.ANY)
    vmem = pl.BlockSpec(memory_space=pltpu.VMEM)
    return pl.pallas_call(
        tile_kernel,
        name="tile",
        out_shape=(
            jax.ShapeDtypeStruct((1024, FEATURE_DIM), BF16),
            jax.ShapeDtypeStruct((1536, FEATURE_DIM), BF16),
            jax.ShapeDtypeStruct((8, ROWS), F32),
        ),
        in_specs=[pl.BlockSpec(memory_space=pltpu.SMEM), vmem] + [any_spec] * len(blocks),
        out_specs=(vmem, vmem, vmem),
        scratch_shapes=[
            pltpu.VMEM((1024, FEATURE_DIM), BF16),
            pltpu.VMEM((1536, FEATURE_DIM), BF16),
            pltpu.VMEM((1024, 1536), BF16),
            pltpu.SemaphoreType.DMA((len(blocks),)),
        ],
        compiler_params=pltpu.CompilerParams(vmem_limit_bytes=48 << 20),
        cost_estimate=pl.CostEstimate(
            flops=6 * 1024 * 1536 * FEATURE_DIM, bytes_accessed=12 << 20, transcendentals=0
        ),
    )(factors, slots, *blocks)


def on_device(images, texts, slot, heat, offset):
    scale = heat[0] / FEATURE_DIM
    factors = jnp.stack([scale * LOG2E, offset[0] * LOG2E, scale])
    at = lax.axis_index("hst")
    x, high = at % 4, at // 4
    places = [high * 4 + (x + step) % 4 for step in (0, -1, 1, 2)]
    wanted = jnp.concatenate(
        [lax.dynamic_slice_in_dim(slot[0], place * ROWS, ROWS) for place in places]
    )
    slots = jnp.stack([wanted - at * ROWS, wanted - (at ^ 4) * ROWS], axis=1)

    image_ring = ring_gather(images, x_step)
    text_ring = ring_gather(texts, q_step)
    other_own = moved(texts, core_step)
    other_far = moved(jnp.concatenate(text_ring[2:]), core_step)
    grad_image, grad_text, loss = tile(
        factors, slots, images, *image_ring, texts, *text_ring, other_own, other_far
    )
    gi = [grad_image[n * ROWS : (n + 1) * ROWS] for n in range(4)]
    gt = [grad_text[n * ROWS : (n + 1) * ROWS] for n in range(6)]
    grad_image = ring_scatter(gi[0], gi[1], gi[2], gi[3], x_step)
    far = summed(gt[3], moved(gt[5], core_step))
    own = gt[0].astype(F32) + moved(gt[4], core_step).astype(F32)
    grad_text = ring_scatter(own, gt[1], gt[2], far, q_step)
    total = loss[0]
    for n, step in ((1, -1), (2, 1), (3, 2)):
        total = total + moved(loss[n], functools.partial(x_step, step))
    return total * (LN2 / 6144), grad_image, grad_text


def solution(mesh):
    in_specs = (P(AXES, None), P(AXES, None), P("dp", None), P(), P())
    out_specs = (P(AXES), P(AXES, None), P(AXES, None))
    return jax.shard_map(
        on_device, mesh=mesh, in_specs=in_specs, out_specs=out_specs, check_vma=False
    )
```

time: 602 us -> 118 us (0.20)
  the two profiles are of different devices: /device:TPU:1 before, /device:TPU:103 now
where the time goes in v1:
time: 118 us
  waiting for transfers between devices  55.7 us (47%)
  starting transfers between devices  29.7 us (25%)
  Pallas kernels  21 us (18%)
  local copies, waits for them, and re-layouts  5.52 us (5%)
  other arithmetic  4.31 us (4%)
  between operations  2.13 us (2%)
    ppermute x23, waiting for transfers between devices, moved(): return lax.ppermute(value, AXES, pairs)  55.7 us
    ppermute x23, starting transfers between devices, moved(): return lax.ppermute(value, AXES, pairs)  29.7 us
    pallas_call x1, Pallas kernels, tile(): pl.pallas_call(tile_kernel, name='tile', out_shape=(jax.ShapeDtypeStruct(...  21 us
    convert_element_type x5, other arithmetic, summed(): return total.astype(BF16)  2.59 us
  transfers between devices with their start and end apart: 23, of which 12 were waited for; matrix products, arithmetic and copies ran while one was open for 6% of the time, Pallas kernels for 0%

profile of v1, /device:TPU:103, one launch (start us, length us, event | category | flops | bytes accessed | tf_op | source)
XLA Modules:
  0.0 118.3 jit_solution(6766228145736939583)
XLA Ops:
  0.6 3.4 %collective-permute-start.5 = (bf16[256,1152]{1,0:T(8,128)(2,1)}, bf16[256,1152]{1,0:T(8,128)(2,1)S(1)}, u32[]{:S(2)}, u32[]{:S(2)}) collective-permute-start(bf16[256,1152]{1,0:T(8,128)(2,1)} %refs_5_.1), channel_id=1, source_target_pairs={{0,252},{1,253},{2,254},{3,255},{4,248},{5,249},{6,250},{7,251},{8... | collective-permute-start | bytes 1769480 | tf_op jit(solution)/shard_map/ppermute | solution.py:49
  4.0 0.0 collective-permute-start.4
  4.0 13.5 %collective-permute-done.5.refs_7_ = bf16[256,1152]{1,0:T(8,128)(2,1)S(1)} collective-permute-done((bf16[256,1152]{1,0:T(8,128)(2,1)}, bf16[256,1152]{1,0:T(8,128)(2,1)S(1)}, u32[]{:S(2)}, u32[]{:S(2)}) %collective-permute-start.5) | collective-permute-done | bytes 589856 | tf_op jit(solution)/shard_map/ppermute | solution.py:49
  17.5 3.7 %collective-permute-start.7 = (bf16[128,1152]{1,0:T(8,128)(2,1)S(1)}, bf16[128,1152]{1,0:T(8,128)(2,1)S(1)}, u32[]{:S(2)}, u32[]{:S(2)}) collective-permute-start(bf16[128,1152]{1,0:T(8,128)(2,1)S(1)} %slice.118), channel_id=1, source_target_pairs={{0,252},{1,253},{2,254},{3,255},{4,248},{5,249},{6,250},{7,251},{8... | collective-permute-start | bytes 884744 | tf_op jit(solution)/shard_map/ppermute | solution.py:49
  21.2 0.0 collective-permute-done.4.refs_6_
  21.2 0.7 slice.117
  21.9 0.2 collective-permute-start
  22.1 1.3 %collective-permute-start.1 = (bf16[256,1152]{1,0:T(8,128)(2,1)}, bf16[256,1152]{1,0:T(8,128)(2,1)S(1)}, u32[]{:S(2)}, u32[]{:S(2)}) collective-permute-start(bf16[256,1152]{1,0:T(8,128)(2,1)} %refs_0_.1), channel_id=1, source_target_pairs={{0,3},{1,0},{2,1},{3,2},{4,7},{5,4},{6,5},{7,6},{8,11},{9,8},{10,9... | collective-permute-start | bytes 1769480 | tf_op jit(solution)/shard_map/ppermute | solution.py:49
  23.4 2.6 %collective-permute-done.7.refs_9_ = bf16[128,1152]{1,0:T(8,128)(2,1)S(1)} collective-permute-done((bf16[128,1152]{1,0:T(8,128)(2,1)S(1)}, bf16[128,1152]{1,0:T(8,128)(2,1)S(1)}, u32[]{:S(2)}, u32[]{:S(2)}) %collective-permute-start.7) | collective-permute-done | bytes 294944 | tf_op jit(solution)/shard_map/ppermute | solution.py:49
  26.0 6.0 %collective-permute-done.6.refs_8_ = bf16[128,1152]{1,0:T(8,128)(2,1)S(1)} collective-permute-done((bf16[128,1152]{1,0:T(8,128)(2,1)}, bf16[128,1152]{1,0:T(8,128)(2,1)S(1)}, u32[]{:S(2)}, u32[]{:S(2)}) %collective-permute-start.6) | collective-permute-done | bytes 294944 | tf_op jit(solution)/shard_map/ppermute | solution.py:49
  32.0 0.9 pad_maximum_fusion
  32.9 4.0 %collective-permute-done.refs_1_ = bf16[256,1152]{1,0:T(8,128)(2,1)S(1)} collective-permute-done((bf16[256,1152]{1,0:T(8,128)(2,1)}, bf16[256,1152]{1,0:T(8,128)(2,1)S(1)}, u32[]{:S(2)}, u32[]{:S(2)}) %collective-permute-start) | collective-permute-done | bytes 589856 | tf_op jit(solution)/shard_map/ppermute | solution.py:49
  36.9 0.7 slice.115
  37.7 1.1 collective-permute-start.2
  38.8 0.7 slice.116
  39.5 0.4 collective-permute-start.3
  41.2 0.2 copy.12.slot_ref
  41.4 0.1 pad_maximum_fusion.5.factors_ref
  41.5 0.0 collective-permute-done.8.refs_10_
  41.5 5.2 %collective-permute-done.2.refs_3_ = bf16[128,1152]{1,0:T(8,128)(2,1)} collective-permute-done((bf16[128,1152]{1,0:T(8,128)(2,1)}, bf16[128,1152]{1,0:T(8,128)(2,1)}, u32[]{:S(2)}, u32[]{:S(2)}) %collective-permute-start.2) | collective-permute-done | bytes 294944 | tf_op jit(solution)/shard_map/ppermute | solution.py:49
  46.7 2.4 %collective-permute-done.3.refs_4_ = bf16[128,1152]{1,0:T(8,128)(2,1)} collective-permute-done((bf16[128,1152]{1,0:T(8,128)(2,1)}, bf16[128,1152]{1,0:T(8,128)(2,1)}, u32[]{:S(2)}, u32[]{:S(2)}) %collective-permute-start.3) | collective-permute-done | bytes 294944 | tf_op jit(solution)/shard_map/ppermute | solution.py:49
  49.1 21.0 %tile.1 = (bf16[1024,1152]{1,0:T(8,128)(2,1)}, bf16[1536,1152]{1,0:T(8,128)(2,1)}, f32[8,256]{1,0:T(8,128)S(1)}) custom-call(f32[3]{0:T(128)S(1)} %pad_maximum_fusion.5.factors_ref, s32[1024,2]{1,0:T(8,128)S(1)} %copy.12.slot_ref, bf16[256,1152]{1,0:T(8,128)(2,1)} %refs_0_.1, bf16[256,1152]{1,0:T(8,128)(2,1)S(1)} %collective-permute-done.refs_1_, ...), custom_call_target="tpu_custom_call" | custom-call | flops 10871635968 | bytes 12582912 | tf_op jit(solution)/shard_map/tile/pallas_call | solution.py:141
  70.1 1.5 %fusion.2 = (bf16[128,1152]{1,0:T(8,128)(2,1)S(1)}, bf16[128,1152]{1,0:T(8,128)(2,1)S(1)}, bf16[128,1152]{1,0:T(8,128)(2,1)S(1)}, bf16[128,1152]{1,0:T(8,128)(2,1)S(1)}) fusion(bf16[1024,1152]{1,0:T(8,128)(2,1)} %get-tuple-element.7), kind=kLoop, calls=%fused_computation.24 | loop fusion | bytes 2359296 | tf_op jit(solution)/shard_map/slice | solution.py:63
  71.6 0.1 collective-permute-start.13
  71.7 1.5 %collective-permute-start.15 = (bf16[128,1152]{1,0:T(8,128)(2,1)S(1)}, bf16[128,1152]{1,0:T(8,128)(2,1)S(1)}, u32[]{:S(2)}, u32[]{:S(2)}) collective-permute-start(bf16[128,1152]{1,0:T(8,128)(2,1)S(1)} %get-tuple-element.20), channel_id=1, source_target_pairs={{0,3},{1,0},{2,1},{3,2},{4,7},{5,4},{6,5},{7,6},{8,11},{9,8},{10,9... | collective-permute-start | bytes 884744 | tf_op jit(solution)/shard_map/ppermute | solution.py:49
  73.1 1.5 %fusion = (bf16[256,1152]{1,0:T(8,128)(2,1)S(1)}, bf16[256,1152]{1,0:T(8,128)(2,1)S(1)}) fusion(bf16[1536,1152]{1,0:T(8,128)(2,1)} %get-tuple-element.8), kind=kLoop, calls=%fused_computation.22 | loop fusion | bytes 2359296 | tf_op jit(solution)/shard_map/slice | solution.py:183
  74.7 2.0 %collective-permute-start.18 = (bf16[256,1152]{1,0:T(8,128)(2,1)S(1)}, bf16[256,1152]{1,0:T(8,128)(2,1)S(1)}, u32[]{:S(2)}, u32[]{:S(2)}) collective-permute-start(bf16[256,1152]{1,0:T(8,128)(2,1)S(1)} %get-tuple-element.12), channel_id=1, source_target_pairs={{0,8},{1,9},{2,10},{3,11},{4,12},{5,13},{6,14},{7,15},{8,0},{9,1},... | collective-permute-start | bytes 1769480 | tf_op jit(solution)/shard_map/ppermute | solution.py:49
  76.7 0.0 collective-permute-start.12
  76.7 1.6 %collective-permute-start.10 = (f32[256]{0:T(256)S(1)}, f32[256]{0:T(256)S(1)}, u32[]{:S(2)}, u32[]{:S(2)}) collective-permute-start(f32[256]{0:T(256)S(1)} %bitcast.14), channel_id=1, source_target_pairs={{0,3},{1,0},{2,1},{3,2},{4,7},{5,4},{6,5},{7,6},{8,11},{9,8},{10,9... | collective-permute-start | bytes 3080 | tf_op jit(solution)/shard_map/ppermute | solution.py:49
  78.3 0.5 collective-permute-done.13
  78.8 1.5 %collective-permute-start.11 = (f32[256]{0:T(256)S(1)}, f32[256]{0:T(256)S(1)}, u32[]{:S(2)}, u32[]{:S(2)}) collective-permute-start(f32[256]{0:T(256)S(1)} %bitcast.13), channel_id=1, source_target_pairs={{0,1},{1,2},{2,3},{3,0},{4,5},{5,6},{6,7},{7,4},{8,9},{9,10},{10,1... | collective-permute-start | bytes 3080 | tf_op jit(solution)/shard_map/ppermute | solution.py:49
  80.3 0.1 add_convert_fusion.6
  80.4 0.2 add_convert_fusion.1
  80.7 1.9 %collective-permute-start.19 = (bf16[128,1152]{1,0:T(8,128)(2,1)S(1)}, bf16[128,1152]{1,0:T(8,128)(2,1)S(1)}, u32[]{:S(2)}, u32[]{:S(2)}) collective-permute-start(bf16[128,1152]{1,0:T(8,128)(2,1)S(1)} %get-tuple-element.23), channel_id=1, source_target_pairs={{0,248},{1,249},{2,250},{3,251},{4,252},{5,253},{6,254},{7,255},{8... | collective-permute-start | bytes 884744 | tf_op jit(solution)/shard_map/ppermute | solution.py:49
  82.5 4.9 %collective-permute-start.21 = (bf16[128,1152]{1,0:T(8,128)(2,1)S(1)}, bf16[128,1152]{1,0:T(8,128)(2,1)S(1)}, u32[]{:S(2)}, u32[]{:S(2)}) collective-permute-start(bf16[128,1152]{1,0:T(8,128)(2,1)S(1)} %get-tuple-element.24), channel_id=1, source_target_pairs={{0,252},{1,253},{2,254},{3,255},{4,248},{5,249},{6,250},{7,251},{8... | collective-permute-start | bytes 884744 | tf_op jit(solution)/shard_map/ppermute | solution.py:49
  87.6 6.2 %collective-permute-done.19 = bf16[128,1152]{1,0:T(8,128)(2,1)S(1)} collective-permute-done((bf16[128,1152]{1,0:T(8,128)(2,1)S(1)}, bf16[128,1152]{1,0:T(8,128)(2,1)S(1)}, u32[]{:S(2)}, u32[]{:S(2)}) %collective-permute-start.19) | collective-permute-done | bytes 294944 | tf_op jit(solution)/shard_map/ppermute | solution.py:49
  93.8 0.3 collective-permute-start.16
  94.0 2.4 %collective-permute-start.14 = (bf16[256,1152]{1,0:T(8,128)(2,1)S(1)}, bf16[256,1152]{1,0:T(8,128)(2,1)S(1)}, u32[]{:S(2)}, u32[]{:S(2)}) collective-permute-start(bf16[256,1152]{1,0:T(8,128)(2,1)S(1)} %pad_maximum_fusion.1), channel_id=1, source_target_pairs={{0,1},{1,2},{2,3},{3,0},{4,5},{5,6},{6,7},{7,4},{8,9},{9,10},{10,1... | collective-permute-start | bytes 1769480 | tf_op jit(solution)/shard_map/ppermute | solution.py:49
  96.5 0.1 add_convert_fusion.4
  96.7 0.1 collective-permute-start.17
  96.8 3.5 %collective-permute-start.22 = (bf16[256,1152]{1,0:T(8,128)(2,1)S(1)}, bf16[256,1152]{1,0:T(8,128)(2,1)S(1)}, u32[]{:S(2)}, u32[]{:S(2)}) collective-permute-start(bf16[256,1152]{1,0:T(8,128)(2,1)S(1)} %pad_maximum_fusion.4), channel_id=1, source_target_pairs={{0,252},{1,253},{2,254},{3,255},{4,248},{5,249},{6,250},{7,251},{8... | collective-permute-start | bytes 1769480 | tf_op jit(solution)/shard_map/ppermute | solution.py:49
  100.4 0.6 add_multiply_fusion
  100.9 7.5 %collective-permute-done.16 = bf16[256,1152]{1,0:T(8,128)(2,1)S(1)} collective-permute-done((bf16[256,1152]{1,0:T(8,128)(2,1)S(1)}, bf16[256,1152]{1,0:T(8,128)(2,1)S(1)}, u32[]{:S(2)}, u32[]{:S(2)}) %collective-permute-start.16) | collective-permute-done | bytes 589856 | tf_op jit(solution)/shard_map/ppermute | solution.py:49
  108.4 0.1 collective-permute-done.14
  108.5 1.0 add_convert_fusion.2
  109.6 4.0 %collective-permute-done.22 = bf16[256,1152]{1,0:T(8,128)(2,1)S(1)} collective-permute-done((bf16[256,1152]{1,0:T(8,128)(2,1)S(1)}, bf16[256,1152]{1,0:T(8,128)(2,1)S(1)}, u32[]{:S(2)}, u32[]{:S(2)}) %collective-permute-start.22) | collective-permute-done | bytes 589856 | tf_op jit(solution)/shard_map/ppermute | solution.py:49
  113.5 3.7 %collective-permute-done.20 = bf16[256,1152]{1,0:T(8,128)(2,1)S(1)} collective-permute-done((bf16[256,1152]{1,0:T(8,128)(2,1)S(1)}, bf16[256,1152]{1,0:T(8,128)(2,1)S(1)}, u32[]{:S(2)}, u32[]{:S(2)}) %collective-permute-start.20) | collective-permute-done | bytes 589856 | tf_op jit(solution)/shard_map/ppermute | solution.py:49
  117.2 1.1 add_convert_fusion
  (31 shorter events, 0.4 us)
Async XLA Ops:
  0.6 32.2 %copy-start.2 = (s32[1,2048]{1,0:T(1,128)S(1)}, s32[1,2048]{1,0:T(1,128)}, u32[]{:S(2)}) copy-start(s32[1,2048]{1,0:T(1,128)} %param.7) | copy-start | bytes 24580
  0.6 16.8 %collective-permute-start.5 = (bf16[256,1152]{1,0:T(8,128)(2,1)}, bf16[256,1152]{1,0:T(8,128)(2,1)S(1)}, u32[]{:S(2)}, u32[]{:S(2)}) collective-permute-start(bf16[256,1152]{1,0:T(8,128)(2,1)} %refs_5_.1), channel_id=1, source_target_pairs={{0,252},{1,253},{2,254},{3,255},{4,248},{5,249},{6,250},{7,251},{8... | collective-permute-start | bytes 1769480 | tf_op jit(solution)/shard_map/ppermute | solution.py:49
  4.0 17.2 %collective-permute-start.4 = (bf16[256,1152]{1,0:T(8,128)(2,1)}, bf16[256,1152]{1,0:T(8,128)(2,1)S(1)}, u32[]{:S(2)}, u32[]{:S(2)}) collective-permute-start(bf16[256,1152]{1,0:T(8,128)(2,1)} %refs_5_.1), channel_id=1, source_target_pairs={{0,248},{1,249},{2,250},{3,251},{4,252},{5,253},{6,254},{7,255},{8... | collective-permute-start | bytes 1769480 | tf_op jit(solution)/shard_map/ppermute | solution.py:49
  17.5 8.5 %collective-permute-start.7 = (bf16[128,1152]{1,0:T(8,128)(2,1)S(1)}, bf16[128,1152]{1,0:T(8,128)(2,1)S(1)}, u32[]{:S(2)}, u32[]{:S(2)}) collective-permute-start(bf16[128,1152]{1,0:T(8,128)(2,1)S(1)} %slice.118), channel_id=1, source_target_pairs={{0,252},{1,253},{2,254},{3,255},{4,248},{5,249},{6,250},{7,251},{8... | collective-permute-start | bytes 884744 | tf_op jit(solution)/shard_map/ppermute | solution.py:49
  21.9 10.1 %collective-permute-start.6 = (bf16[128,1152]{1,0:T(8,128)(2,1)}, bf16[128,1152]{1,0:T(8,128)(2,1)S(1)}, u32[]{:S(2)}, u32[]{:S(2)}) collective-permute-start(bf16[128,1152]{1,0:T(8,128)(2,1)} %slice.117), channel_id=1, source_target_pairs={{0,248},{1,249},{2,250},{3,251},{4,252},{5,253},{6,254},{7,255},{8... | collective-permute-start | bytes 884744 | tf_op jit(solution)/shard_map/ppermute | solution.py:49
  21.9 15.0 %collective-permute-start = (bf16[256,1152]{1,0:T(8,128)(2,1)}, bf16[256,1152]{1,0:T(8,128)(2,1)S(1)}, u32[]{:S(2)}, u32[]{:S(2)}) collective-permute-start(bf16[256,1152]{1,0:T(8,128)(2,1)} %refs_0_.1), channel_id=1, source_target_pairs={{0,1},{1,2},{2,3},{3,0},{4,5},{5,6},{6,7},{7,4},{8,9},{9,10},{10,1... | collective-permute-start | bytes 1769480 | tf_op jit(solution)/shard_map/ppermute | solution.py:49
  22.1 16.7 %collective-permute-start.1 = (bf16[256,1152]{1,0:T(8,128)(2,1)}, bf16[256,1152]{1,0:T(8,128)(2,1)S(1)}, u32[]{:S(2)}, u32[]{:S(2)}) collective-permute-start(bf16[256,1152]{1,0:T(8,128)(2,1)} %refs_0_.1), channel_id=1, source_target_pairs={{0,3},{1,0},{2,1},{3,2},{4,7},{5,4},{6,5},{7,6},{8,11},{9,8},{10,9... | collective-permute-start | bytes 1769480 | tf_op jit(solution)/shard_map/ppermute | solution.py:49
  23.4 18.1 %collective-permute-start.8 = (bf16[256,1152]{1,0:T(8,128)(2,1)}, bf16[256,1152]{1,0:T(8,128)(2,1)}, u32[]{:S(2)}, u32[]{:S(2)}) collective-permute-start(bf16[256,1152]{1,0:T(8,128)(2,1)} %refs_5_.1), channel_id=1, source_target_pairs={{0,8},{1,9},{2,10},{3,11},{4,12},{5,13},{6,14},{7,15},{8,0},{9,1},... | collective-permute-start | bytes 1769480 | tf_op jit(solution)/shard_map/ppermute | solution.py:49
  32.8 16.3 %collective-permute-start.9 = (bf16[256,1152]{1,0:T(8,128)(2,1)}, bf16[256,1152]{1,0:T(8,128)(2,1)}, u32[]{:S(2)}, u32[]{:S(2)}) collective-permute-start(bf16[256,1152]{1,0:T(8,128)(2,1)} %pad_maximum_fusion), channel_id=1, source_target_pairs={{0,8},{1,9},{2,10},{3,11},{4,12},{5,13},{6,14},{7,15},{8,0},{9,1},... | collective-permute-start | bytes 1769480 | tf_op jit(solution)/shard_map/ppermute | solution.py:49
  37.7 9.0 %collective-permute-start.2 = (bf16[128,1152]{1,0:T(8,128)(2,1)}, bf16[128,1152]{1,0:T(8,128)(2,1)}, u32[]{:S(2)}, u32[]{:S(2)}) collective-permute-start(bf16[128,1152]{1,0:T(8,128)(2,1)} %slice.115), channel_id=1, source_target_pairs={{0,1},{1,2},{2,3},{3,0},{4,5},{5,6},{6,7},{7,4},{8,9},{9,10},{10,1... | collective-permute-start | bytes 884744 | tf_op jit(solution)/shard_map/ppermute | solution.py:49
  39.5 9.6 %collective-permute-start.3 = (bf16[128,1152]{1,0:T(8,128)(2,1)}, bf16[128,1152]{1,0:T(8,128)(2,1)}, u32[]{:S(2)}, u32[]{:S(2)}) collective-permute-start(bf16[128,1152]{1,0:T(8,128)(2,1)} %slice.116), channel_id=1, source_target_pairs={{0,3},{1,0},{2,1},{3,2},{4,7},{5,4},{6,5},{7,6},{8,11},{9,8},{10,9... | collective-permute-start | bytes 884744 | tf_op jit(solution)/shard_map/ppermute | solution.py:49
  70.1 4.5 %copy-start = (bf16[1536,1152]{1,0:T(8,128)(2,1)S(1)}, bf16[1536,1152]{1,0:T(8,128)(2,1)}, u32[]{:S(2)}) copy-start(bf16[1536,1152]{1,0:T(8,128)(2,1)} %get-tuple-element.8) | copy-start | bytes 10616836
  71.6 7.2 %collective-permute-start.13 = (bf16[128,1152]{1,0:T(8,128)(2,1)S(1)}, bf16[128,1152]{1,0:T(8,128)(2,1)S(1)}, u32[]{:S(2)}, u32[]{:S(2)}) collective-permute-start(bf16[128,1152]{1,0:T(8,128)(2,1)S(1)} %get-tuple-element.19), channel_id=1, source_target_pairs={{0,1},{1,2},{2,3},{3,0},{4,5},{5,6},{6,7},{7,4},{8,9},{9,10},{10,1... | collective-permute-start | bytes 884744 | tf_op jit(solution)/shard_map/ppermute | solution.py:49
  71.7 8.6 %collective-permute-start.15 = (bf16[128,1152]{1,0:T(8,128)(2,1)S(1)}, bf16[128,1152]{1,0:T(8,128)(2,1)S(1)}, u32[]{:S(2)}, u32[]{:S(2)}) collective-permute-start(bf16[128,1152]{1,0:T(8,128)(2,1)S(1)} %get-tuple-element.20), channel_id=1, source_target_pairs={{0,3},{1,0},{2,1},{3,2},{4,7},{5,4},{6,5},{7,6},{8,11},{9,8},{10,9... | collective-permute-start | bytes 884744 | tf_op jit(solution)/shard_map/ppermute | solution.py:49
  73.1 7.2 %copy-start.1 = (bf16[1024,1152]{1,0:T(8,128)(2,1)S(1)}, bf16[1024,1152]{1,0:T(8,128)(2,1)}, u32[]{:S(2)}) copy-start(bf16[1024,1152]{1,0:T(8,128)(2,1)} %get-tuple-element.7) | copy-start | bytes 7077892
  74.7 5.8 %collective-permute-start.18 = (bf16[256,1152]{1,0:T(8,128)(2,1)S(1)}, bf16[256,1152]{1,0:T(8,128)(2,1)S(1)}, u32[]{:S(2)}, u32[]{:S(2)}) collective-permute-start(bf16[256,1152]{1,0:T(8,128)(2,1)S(1)} %get-tuple-element.12), channel_id=1, source_target_pairs={{0,8},{1,9},{2,10},{3,11},{4,12},{5,13},{6,14},{7,15},{8,0},{9,1},... | collective-permute-start | bytes 1769480 | tf_op jit(solution)/shard_map/ppermute | solution.py:49
  76.7 20.0 %collective-permute-start.12 = (f32[256]{0:T(256)S(1)}, f32[256]{0:T(256)S(1)}, u32[]{:S(2)}, u32[]{:S(2)}) collective-permute-start(f32[256]{0:T(256)S(1)} %bitcast.15), channel_id=1, source_target_pairs={{0,2},{1,3},{2,0},{3,1},{4,6},{5,7},{6,4},{7,5},{8,10},{9,11},{10,... | collective-permute-start | bytes 3080 | tf_op jit(solution)/shard_map/ppermute | solution.py:49
  76.7 20.1 %collective-permute-start.10 = (f32[256]{0:T(256)S(1)}, f32[256]{0:T(256)S(1)}, u32[]{:S(2)}, u32[]{:S(2)}) collective-permute-start(f32[256]{0:T(256)S(1)} %bitcast.14), channel_id=1, source_target_pairs={{0,3},{1,0},{2,1},{3,2},{4,7},{5,4},{6,5},{7,6},{8,11},{9,8},{10,9... | collective-permute-start | bytes 3080 | tf_op jit(solution)/shard_map/ppermute | solution.py:49
  78.8 21.6 %collective-permute-start.11 = (f32[256]{0:T(256)S(1)}, f32[256]{0:T(256)S(1)}, u32[]{:S(2)}, u32[]{:S(2)}) collective-permute-start(f32[256]{0:T(256)S(1)} %bitcast.13), channel_id=1, source_target_pairs={{0,1},{1,2},{2,3},{3,0},{4,5},{5,6},{6,7},{7,4},{8,9},{9,10},{10,1... | collective-permute-start | bytes 3080 | tf_op jit(solution)/shard_map/ppermute | solution.py:49
  80.7 13.1 %collective-permute-start.19 = (bf16[128,1152]{1,0:T(8,128)(2,1)S(1)}, bf16[128,1152]{1,0:T(8,128)(2,1)S(1)}, u32[]{:S(2)}, u32[]{:S(2)}) collective-permute-start(bf16[128,1152]{1,0:T(8,128)(2,1)S(1)} %get-tuple-element.23), channel_id=1, source_target_pairs={{0,248},{1,249},{2,250},{3,251},{4,252},{5,253},{6,254},{7,255},{8... | collective-permute-start | bytes 884744 | tf_op jit(solution)/shard_map/ppermute | solution.py:49
  82.5 11.5 %collective-permute-start.21 = (bf16[128,1152]{1,0:T(8,128)(2,1)S(1)}, bf16[128,1152]{1,0:T(8,128)(2,1)S(1)}, u32[]{:S(2)}, u32[]{:S(2)}) collective-permute-start(bf16[128,1152]{1,0:T(8,128)(2,1)S(1)} %get-tuple-element.24), channel_id=1, source_target_pairs={{0,252},{1,253},{2,254},{3,255},{4,248},{5,249},{6,250},{7,251},{8... | collective-permute-start | bytes 884744 | tf_op jit(solution)/shard_map/ppermute | solution.py:49
  93.8 14.7 %collective-permute-start.16 = (bf16[256,1152]{1,0:T(8,128)(2,1)S(1)}, bf16[256,1152]{1,0:T(8,128)(2,1)S(1)}, u32[]{:S(2)}, u32[]{:S(2)}) collective-permute-start(bf16[256,1152]{1,0:T(8,128)(2,1)S(1)} %pad_maximum_fusion.2), channel_id=1, source_target_pairs={{0,3},{1,0},{2,1},{3,2},{4,7},{5,4},{6,5},{7,6},{8,11},{9,8},{10,9... | collective-permute-start | bytes 1769480 | tf_op jit(solution)/shard_map/ppermute | solution.py:49
  94.0 14.5 %collective-permute-start.14 = (bf16[256,1152]{1,0:T(8,128)(2,1)S(1)}, bf16[256,1152]{1,0:T(8,128)(2,1)S(1)}, u32[]{:S(2)}, u32[]{:S(2)}) collective-permute-start(bf16[256,1152]{1,0:T(8,128)(2,1)S(1)} %pad_maximum_fusion.1), channel_id=1, source_target_pairs={{0,1},{1,2},{2,3},{3,0},{4,5},{5,6},{6,7},{7,4},{8,9},{9,10},{10,1... | collective-permute-start | bytes 1769480 | tf_op jit(solution)/shard_map/ppermute | solution.py:49
  96.7 12.8 %collective-permute-start.17 = (bf16[256,1152]{1,0:T(8,128)(2,1)S(1)}, bf16[256,1152]{1,0:T(8,128)(2,1)S(1)}, u32[]{:S(2)}, u32[]{:S(2)}) collective-permute-start(bf16[256,1152]{1,0:T(8,128)(2,1)S(1)} %get-tuple-element.11), channel_id=1, source_target_pairs={{0,8},{1,9},{2,10},{3,11},{4,12},{5,13},{6,14},{7,15},{8,0},{9,1},... | collective-permute-start | bytes 1769480 | tf_op jit(solution)/shard_map/ppermute | solution.py:49
  96.8 16.7 %collective-permute-start.22 = (bf16[256,1152]{1,0:T(8,128)(2,1)S(1)}, bf16[256,1152]{1,0:T(8,128)(2,1)S(1)}, u32[]{:S(2)}, u32[]{:S(2)}) collective-permute-start(bf16[256,1152]{1,0:T(8,128)(2,1)S(1)} %pad_maximum_fusion.4), channel_id=1, source_target_pairs={{0,252},{1,253},{2,254},{3,255},{4,248},{5,249},{6,250},{7,251},{8... | collective-permute-start | bytes 1769480 | tf_op jit(solution)/shard_map/ppermute | solution.py:49
  100.4 16.8 %collective-permute-start.20 = (bf16[256,1152]{1,0:T(8,128)(2,1)S(1)}, bf16[256,1152]{1,0:T(8,128)(2,1)S(1)}, u32[]{:S(2)}, u32[]{:S(2)}) collective-permute-start(bf16[256,1152]{1,0:T(8,128)(2,1)S(1)} %pad_maximum_fusion.3), channel_id=1, source_target_pairs={{0,248},{1,249},{2,250},{3,251},{4,252},{5,253},{6,254},{7,255},{8... | collective-permute-start | bytes 1769480 | tf_op jit(solution)/shard_map/ppermute | solution.py:49

commit v2 on v0

v2 whole, which is shorter than its diff:
```python
import functools

import jax
import jax.numpy as jnp
from jax import lax
from jax.experimental import pallas as pl
from jax.experimental.pallas import tpu as pltpu
from jax.sharding import PartitionSpec as P

FEATURE_DIM = 1152
ROWS = 256
LOG2E = 1.4426950408889634
LN2 = 0.6931471805599453
HBM = pl.BlockSpec(memory_space=pltpu.HBM)
VMEM = pl.BlockSpec(memory_space=pltpu.VMEM)
SMEM = pl.BlockSpec(memory_space=pltpu.SMEM)
NT = (((1,), (1,)), ((), ()))
TN = (((0,), (0,)), ((), ()))
STEPS = {"i0": 0, "i1": -1, "i2": 1, "i3": 2}
IMAGES = list(STEPS)
TEXTS = ["t0", "t1", "t2", "t3", "c0", "c3"]
HOMES = {"t0": 0, "t3": 4}
AXES = ("dp", "hst")
F32 = jnp.float32
BF16 = jnp.bfloat16


def place_of(index):
    dp, hst = divmod(index, 8)
    return hst % 4, (hst // 4) * 2 + (dp // 2) % 2, dp // 4, dp % 2


def index_of(x, y, z, core):
    x, y, z = x % 4, y % 4, z % 8
    return (z * 4 + (y % 2) * 2 + core) * 8 + (y // 2) * 4 + x


def x_step(steps, x, y, z, core):
    return x + (steps if core == 0 else -steps), y, z, core


def q_step(steps, x, y, z, core):
    in_plane = y % 2 != core
    if not in_plane:
        z = z - 1 if core == 0 else z + 1
    return x, y + (steps if in_plane else -steps), z, 1 - core


def core_step(x, y, z, core):
    return x, y, z, 1 - core


def moved(value, step):
    pairs = [(i, index_of(*step(*place_of(i)))) for i in range(256)]
    return lax.ppermute(value, AXES, pairs)


def pair_terms(product, factors, positive):
    z = product * factors[0] + factors[1]
    if positive is not None:
        z = jnp.where(positive, -z, z)
    e = jnp.exp2(-jnp.abs(z))
    u = 1.0 + e
    log_u = jnp.where(e < 2.0**-8, LOG2E * e * (1.0 - 0.5 * e), jnp.log2(u))
    softplus = jnp.maximum(z, 0.0) + log_u
    scale = factors[2]
    coefficient = jnp.where(z >= 0.0, scale, scale * e) * pltpu.reciprocal(u, approx=True)
    if positive is not None:
        coefficient = jnp.where(positive, -coefficient, coefficient)
    return coefficient, softplus


def pairs_kernel(plan, at_ref, factors_ref, slot_ref, *refs):
    pairs, image_names, text_names, old_names, loss_names, kept, framed = plan
    refs = list(refs)

    def take(names):
        return {name: refs.pop(0) for name in names}

    images, texts = take(image_names), take(text_names)
    old, losses = take(old_names), take(loss_names)
    new = take(image_names + text_names)
    copies = take(kept)
    (loss_out, coef) = refs
    for name in kept:
        copies[name][...] = {**images, **texts}[name][...]
    factors = [factors_ref[n] for n in range(3)]
    at = at_ref[0]
    columns = lax.broadcasted_iota(jnp.int32, (ROWS, ROWS), 1)
    sums, wanted = {}, {}

    def block(names, name):
        return pl.ds(names.index(name) * ROWS, ROWS)

    def place_wanted(i):
        if i not in wanted:
            place = ((at & 4) + ((at + STEPS[i] * at_ref[1]) & 3)) * ROWS
            row = slot_ref[:, pl.ds(pl.multiple_of(place, ROWS), ROWS)]
            wanted[i] = jnp.broadcast_to(row, (128, ROWS)).T[:, :1]
        return wanted[i]

    def spot(i, t):
        return coef.at[block(image_names, i), block(text_names, t)]

    for i, t in pairs:
        product = lax.dot_general(
            images[i][...], texts[t][...], NT, preferred_element_type=F32
        )
        positive = None
        if t in HOMES:
            positive = columns == place_wanted(i) - (at ^ HOMES[t]) * ROWS
        coefficient, softplus = pair_terms(product, factors, positive)
        spot(i, t)[...] = coefficient.astype(BF16)
        part = softplus[:, :128] + softplus[:, 128:]
        sums[i] = part if i not in sums else sums[i] + part

    for t in text_names:
        mine = [i for i in image_names if (i, t) in pairs]
        total = lax.dot_general(
            jnp.concatenate([spot(i, t)[...] for i in mine]),
            jnp.concatenate([images[i][...] for i in mine]),
            TN,
            preferred_element_type=F32,
        )
        if t in old:
            total = total + old[t][...].astype(F32)
        if "more" in old:
            total = total + old["more"][...].astype(F32)
        new[t][...] = total.astype(BF16)
    for n, i in enumerate(IMAGES):
        row = pl.ds(n, 1)
        if i not in sums:
            value = sum((ref[row, :] for ref in losses.values()), jnp.zeros((1, ROWS), F32))
            loss_out[row, :] = value
            continue
        mine = [t for t in text_names if (i, t) in pairs]
        total = jnp.dot(
            jnp.concatenate([spot(i, t)[...] for t in mine], axis=1),
            jnp.concatenate([texts[t][...] for t in mine]),
            preferred_element_type=F32,
        )
        if i in old:
            total = total + old[i][...].astype(F32)
        new[i][pl.ds(0, ROWS), :] = total.astype(BF16)
        value = jnp.sum(sums[i].T, axis=0, keepdims=True)
        value = sum((ref[row, :] for ref in losses.values()), value)
        loss_out[row, :] = value
        if i in framed:
            at_row = lax.broadcasted_iota(jnp.int32, (16, ROWS), 0)
            large = value.astype(BF16).astype(F32)
            both = jnp.where(at_row == 0, large, jnp.where(at_row == 1, value - large, 0.0))
            new[i][pl.ds(ROWS, 16), :] = jnp.zeros((16, FEATURE_DIM), BF16)
            new[i][pl.ds(ROWS, 16), pl.ds(0, ROWS)] = both.astype(BF16)


def pair_call(name, common, values, pairs, old=None, losses=(), kept=(), framed=()):
    old = old or {}
    image_names = [i for i in IMAGES if any(i == p[0] for p in pairs)]
    text_names = [t for t in TEXTS if any(t == p[1] for p in pairs)]
    old_names = [n for n in [*image_names, *text_names, "more"] if n in old]
    plan = (pairs, image_names, text_names, old_names, list(range(len(losses))), kept, framed)
    blocks = [values[n] for n in image_names + text_names] + [old[n] for n in old_names]
    names = [*image_names, *text_names, *kept]
    rows = [ROWS + 16 if n in framed else ROWS for n in image_names] + [ROWS] * (
        len(text_names) + len(kept)
    )
    out = pl.pallas_call(
        functools.partial(pairs_kernel, plan),
        name=name,
        out_shape=[jax.ShapeDtypeStruct((r, FEATURE_DIM), BF16) for r in rows]
        + [jax.ShapeDtypeStruct((8, ROWS), F32)],
        in_specs=[SMEM, SMEM, VMEM] + [VMEM] * (len(blocks) + len(losses)),
        out_specs=[VMEM] * (len(rows) + 1),
        scratch_shapes=[pltpu.VMEM((len(image_names) * ROWS, len(text_names) * ROWS), BF16)],
        compiler_params=pltpu.CompilerParams(vmem_limit_bytes=24 << 20),
        cost_estimate=pl.CostEstimate(
            flops=6 * len(pairs) * ROWS * ROWS * FEATURE_DIM,
            bytes_accessed=2 * ROWS * FEATURE_DIM * (len(blocks) + len(rows)),
            transcendentals=0,
        ),
    )(*common, *blocks, *losses)
    grads = dict(zip(image_names + text_names, out))
    return {**old, **grads}, out[-1], list(out[len(image_names) + len(text_names) : -1])


def joined_kernel(left, right, out):
    rows = pl.ds(0, ROWS)
    out[rows, :] = (left[rows, :].astype(F32) + right[rows, :].astype(F32)).astype(BF16)
    if out.shape[0] > ROWS:
        rows = pl.ds(ROWS, 16)
        both = left[rows, :].astype(F32) + right[rows, :].astype(F32)
        value = both[0:1] + both[1:2]
        at_row = lax.broadcasted_iota(jnp.int32, both.shape, 0)
        large = value.astype(BF16).astype(F32)
        out[rows, :] = jnp.where(
            at_row == 0, large, jnp.where(at_row == 1, value - large, 0.0)
        ).astype(BF16)


def joined(left, right):
    return pl.pallas_call(
        joined_kernel,
        name="joined",
        out_shape=jax.ShapeDtypeStruct(left.shape, BF16),
        in_specs=[VMEM, VMEM],
        out_specs=VMEM,
        compiler_params=pltpu.CompilerParams(vmem_limit_bytes=16 << 20),
        cost_estimate=pl.CostEstimate(
            flops=ROWS * FEATURE_DIM, bytes_accessed=6 * ROWS * FEATURE_DIM, transcendentals=0
        ),
    )(left, right)


def summed(*terms):
    total = terms[0][:ROWS].astype(F32)
    for term in terms[1:]:
        total = total + term[:ROWS].astype(F32)
    return total.astype(BF16)


def tied(value, *others):
    return lax.optimization_barrier((value, *others))[0]


def on_device(images, texts, slot, heat, offset):
    scale = heat[0] / FEATURE_DIM
    factors = jnp.stack([scale * LOG2E, offset[0] * LOG2E, scale])
    way = 1 - 2 * (lax.axis_index("dp") & 1)
    at = jnp.stack([lax.axis_index("hst"), way]).astype(jnp.int32)
    call = functools.partial(pair_call, common=(at, factors, slot))

    def xs(value, n):
        with jax.named_scope("x"):
            return moved(value, functools.partial(x_step, n))

    def qs(value, n):
        with jax.named_scope("q"):
            return moved(value, functools.partial(q_step, n))

    def across(value):
        with jax.named_scope("core"):
            return moved(value, core_step)

    v = {"i0": images, "t0": texts}
    v["t1"], v["i1"] = qs(texts, 1), xs(images, 1)
    v["t2"], v["i2"] = qs(texts, -1), xs(images, -1)
    v["c0"] = across(texts)
    g, loss, (v["i0"], v["t0"]) = call(
        "own", values=v, pairs=[("i0", "t0"), ("i0", "c0")], kept=("i0", "t0")
    )
    v["t3"] = qs(tied(v["t1"], loss), 1)
    v["i3"] = xs(tied(v["i1"], loss), 1)
    g, loss, _ = call(
        "near", values=v, old=g, losses=(loss,),
        pairs=[("i1", "t1"), ("i1", "t2"), ("i2", "t1"), ("i2", "t2"), ("i0", "t1"),
               ("i0", "t2"), ("i1", "t0"), ("i1", "c0"), ("i2", "t0"), ("i2", "c0")],
    )
    v["c3"] = across(tied(v["t3"], loss))
    g, loss, _ = call(
        "third", values=v, old=g, losses=(loss,),
        pairs=[("i3", t) for t in ("t1", "t2", "t0", "c0")],
    )
    from_next = qs(g["t1"], -1)
    from_core = across(g["c0"])
    g, loss, _ = call(
        "across", values=v, old=g, losses=(loss,), pairs=[(i, "c3") for i in IMAGES]
    )
    far_core = across(g["c3"])
    g, loss, _ = call(
        "far", values=v, old=g, losses=(loss,), pairs=[("i3", "t3"), ("i1", "t3")],
        framed=("i1", "i3"),
    )
    image_far = xs(g["i3"], 1)
    image_next = xs(g["i1"], -1)
    g, loss, _ = call(
        "rest", values=v, old={**g, "more": far_core}, losses=(loss,),
        pairs=[("i0", "t3"), ("i2", "t3")], framed=("i2",),
    )
    text_far = qs(g["t3"], 1)
    text_prev = qs(joined(g["t2"], text_far), 1)
    image_prev = xs(joined(g["i2"], tied(image_far, text_far)), 1)
    row_loss = loss[0]
    for s in (image_next, image_prev):
        row_loss = row_loss + s[ROWS, :ROWS].astype(F32) + s[ROWS + 1, :ROWS].astype(F32)
    grad_image = summed(g["i0"], image_next, image_prev)
    grad_text = summed(g["t0"], from_core, from_next, text_prev)
    return row_loss * (LN2 / 6144), grad_image, grad_text


def solution(mesh):
    in_specs = (P(AXES, None), P(AXES, None), P("dp", None), P(), P())
    out_specs = (P(AXES), P(AXES, None), P(AXES, None))
    return jax.shard_map(
        on_device, mesh=mesh, in_specs=in_specs, out_specs=out_specs, check_vma=False
    )
```

time: 602 us -> 84.6 us (0.14)
  waiting for transfers between devices: 534 us -> 35.5 us
  matrix products: 41.5 us -> 0 us
  Pallas kernels: 0 us -> 21 us
  starting transfers between devices: 3.96 us -> 20.1 us
  between operations: 15.1 us -> 2.07 us
    reduce_scatter x3 -> x0, waiting for transfers between devices: 306 us -> none  [the longest x1 132 us: on_device(): lax.psum_scatter(low_text, 'hst', scatter_dimension=0, tiled=True)]
    ppermute x4 -> x16, waiting for transfers between devices: 141 us -> 35.5 us  [moved(): return lax.ppermute(value, AXES, pairs)]
    all_gather x1 -> x0, waiting for transfers between devices: 87.1 us -> none  [on_device(): own_block = lax.all_gather(caption_features, 'hst', axis=0, tiled=True)]
    dot_general x9 -> x0, matrix products: 41.5 us -> none  [the longest x3 16.7 us: text_terms(): lax.dot_general(coefficient, image_rows, (((0,), (0,)), ((), ())), prefer...]
    pallas_call x0 -> x8, Pallas kernels: none -> 21 us  [the longest x6 20.7 us: pair_call(): pl.pallas_call(functools.partial(pairs_kernel, plan), name=name, out_shap...]
    ppermute x4 -> x16, starting transfers between devices: 3.62 us -> 20.1 us  [moved(): return lax.ppermute(value, AXES, pairs)]
  transfers between devices with their start and end apart: 8 -> 16, of which waited for: 6 -> 6; matrix products, arithmetic and copies ran while one was open for 6% -> 1% of each run, Pallas kernels for 0% -> 18%
where the time goes in v2:
time: 84.6 us; the launch traced here: 84.4 us
  waiting for transfers between devices  35.5 us (42%)
  Pallas kernels  21 us (25%)
  starting transfers between devices  20.1 us (24%)
  other arithmetic  2.87 us (3%)
  local copies, waits for them, and re-layouts  2.83 us (3%)
  between operations  2.07 us (2%)
    ppermute x16, waiting for transfers between devices, moved(): return lax.ppermute(value, AXES, pairs)  35.5 us
    pallas_call x6, Pallas kernels, pair_call(): pl.pallas_call(functools.partial(pairs_kernel, plan), name=name, out_shap...  20.7 us
    ppermute x16, starting transfers between devices, moved(): return lax.ppermute(value, AXES, pairs)  20.1 us
    unnamed x6, local copies, waits for them, and re-layouts  2.83 us
    convert_element_type x2, other arithmetic, summed(): return total.astype(BF16)  2.15 us
  transfers between devices with their start and end apart: 16, of which 6 were waited for; matrix products, arithmetic and copies ran while one was open for 1% of the time, Pallas kernels for 18%

profile of v2, /device:TPU:1, one launch (start us, length us, event | category | flops | bytes accessed | tf_op | source)
XLA Modules:
  0.0 84.4 jit_solution(15995113198394166673)
XLA Ops:
  0.6 3.3 %collective-permute-start = (bf16[256,1152]{1,0:T(8,128)(2,1)}, bf16[256,1152]{1,0:T(8,128)(2,1)S(1)}, u32[]{:S(2)}, u32[]{:S(2)}) collective-permute-start(bf16[256,1152]{1,0:T(8,128)(2,1)} %refs_1_.1), channel_id=1, source_target_pairs={{0,8},{1,9},{2,10},{3,11},{4,12},{5,13},{6,14},{7,15},{8,0},{9,1},... | collective-permute-start | bytes 1769480 | tf_op jit(solution)/shard_map/core/ppermute | solution.py:55
  4.0 0.0 collective-permute-start.2
  4.0 2.0 %collective-permute-start.4 = (bf16[256,1152]{1,0:T(8,128)(2,1)}, bf16[256,1152]{1,0:T(8,128)(2,1)S(1)}, u32[]{:S(2)}, u32[]{:S(2)}) collective-permute-start(bf16[256,1152]{1,0:T(8,128)(2,1)} %refs_0_.1), channel_id=1, source_target_pairs={{0,1},{1,2},{2,3},{3,0},{4,5},{5,6},{6,7},{7,4},{8,11},{9,8},{10,9... | collective-permute-start | bytes 1769480 | tf_op jit(solution)/shard_map/x/ppermute | solution.py:55
  6.0 0.0 collective-permute-start.1
  6.0 4.2 %collective-permute-start.6 = (bf16[256,1152]{1,0:T(8,128)(2,1)}, bf16[256,1152]{1,0:T(8,128)(2,1)S(1)}, u32[]{:S(2)}, u32[]{:S(2)}) collective-permute-start(bf16[256,1152]{1,0:T(8,128)(2,1)} %refs_1_.1), channel_id=1, source_target_pairs={{0,248},{1,249},{2,250},{3,251},{4,252},{5,253},{6,254},{7,255},{8... | collective-permute-start | bytes 1769480 | tf_op jit(solution)/shard_map/q/ppermute | solution.py:55
  11.4 0.1 pad_add_fusion.at_ref
  11.5 0.1 pad_maximum_fusion.factors_ref
  11.6 0.0 collective-permute-done.refs_2_.refs_6_.refs_4_
  11.6 0.7 copy-done
  12.3 1.1 %copy-done.1 = bf16[256,1152]{1,0:T(8,128)(2,1)S(1)} copy-done((bf16[256,1152]{1,0:T(8,128)(2,1)S(1)}, bf16[256,1152]{1,0:T(8,128)(2,1)}, u32[]{:S(2)}) %copy-start.1) | copy-done | bytes 589848
  13.4 1.1 %copy-done.2 = bf16[256,1152]{1,0:T(8,128)(2,1)S(1)} copy-done((bf16[256,1152]{1,0:T(8,128)(2,1)S(1)}, bf16[256,1152]{1,0:T(8,128)(2,1)}, u32[]{:S(2)}) %copy-start.2) | copy-done | bytes 589848
  14.4 2.2 %own.1 = (bf16[256,1152]{1,0:T(8,128)(2,1)S(1)}, bf16[256,1152]{1,0:T(8,128)(2,1)S(1)}, bf16[256,1152]{1,0:T(8,128)(2,1)S(1)}, bf16[256,1152]{1,0:T(8,128)(2,1)S...) custom-call(s32[2]{0:T(128)S(1)} %pad_add_fusion.at_ref, f32[3]{0:T(128)S(1)} %pad_maximum_fusion.factors_ref, ...), custom_call_target="tpu_custom_call" | custom-call | flops 905969664 | bytes 4718592 | tf_op jit(solution)/shard_map/own/pallas_call | solution.py:167
  16.7 0.0 collective-permute-done.2.refs_4_.refs_2_
  16.7 0.1 collective-permute-start.3
  16.8 0.0 collective-permute-done.4.refs_1_.refs_0_
  16.8 0.3 collective-permute-start.5
  17.1 0.5 collective-permute-done.1.refs_2_.refs_1_
  17.6 5.2 %collective-permute-done.6.refs_5_.refs_3_ = bf16[256,1152]{1,0:T(8,128)(2,1)S(1)} collective-permute-done((bf16[256,1152]{1,0:T(8,128)(2,1)}, bf16[256,1152]{1,0:T(8,128)(2,1)S(1)}, u32[]{:S(2)}, u32[]{:S(2)}) %collective-permute-start.6) | collective-permute-done | bytes 589856 | tf_op jit(solution)/shard_map/q/ppermute | solution.py:55
  22.7 7.1 %near.1 = (bf16[256,1152]{1,0:T(8,128)(2,1)S(1)}, bf16[256,1152]{1,0:T(8,128)(2,1)S(1)}, bf16[256,1152]{1,0:T(8,128)(2,1)S(1)}, bf16[256,1152]{1,0:T(8,128)(2,1)...) custom-call(s32[2]{0:T(128)S(1)} %pad_add_fusion.at_ref, ...), custom_call_target="tpu_custom_call" | custom-call | flops 4529848320 | bytes 10027008 | tf_op jit(solution)/shard_map/near/pallas_call | solution.py:167
  29.9 2.8 %collective-permute-done.3.refs_2_ = bf16[256,1152]{1,0:T(8,128)(2,1)S(1)} collective-permute-done((bf16[256,1152]{1,0:T(8,128)(2,1)S(1)}, bf16[256,1152]{1,0:T(8,128)(2,1)S(1)}, u32[]{:S(2)}, u32[]{:S(2)}) %collective-permute-start.3) | collective-permute-done | bytes 589856 | tf_op jit(solution)/shard_map/q/ppermute | solution.py:55
  32.6 1.4 %collective-permute-start.7 = (bf16[256,1152]{1,0:T(8,128)(2,1)S(1)}, bf16[256,1152]{1,0:T(8,128)(2,1)S(1)}, u32[]{:S(2)}, u32[]{:S(2)}) collective-permute-start(bf16[256,1152]{1,0:T(8,128)(2,1)S(1)} %collective-permute-done.3.refs_2_), channel_id=1, source_target_pairs={{0,8},{1,9},{2,10},{3,11},{4,12},{5,13},{6,14},{7,15},{8,0},{9,1},... | collective-permute-start | bytes 1769480 | tf_op jit(solution)/shard_map/core/ppermute | solution.py:55
  34.1 0.0 collective-permute-done.5.refs_0_.refs_3_.refs_1_
  34.1 3.5 %third.1 = (bf16[256,1152]{1,0:T(8,128)(2,1)S(1)}, bf16[256,1152]{1,0:T(8,128)(2,1)S(1)}, bf16[256,1152]{1,0:T(8,128)(2,1)S(1)}, bf16[256,1152]{1,0:T(8,128)(2,1...) custom-call(s32[2]{0:T(128)S(1)} %pad_add_fusion.at_ref, f32[3]{0:T(128)S(1)} %pad_maximum_fusion.factors_ref, ...), custom_call_target="tpu_custom_call" | custom-call | flops 1811939328 | bytes 8257536 | tf_op jit(solution)/shard_map/third/pallas_call | solution.py:167
  37.6 0.0 collective-permute-done.7.refs_4_
  37.6 3.2 %across.1 = (bf16[256,1152]{1,0:T(8,128)(2,1)S(1)}, bf16[256,1152]{1,0:T(8,128)(2,1)S(1)}, bf16[256,1152]{1,0:T(8,128)(2,1)S(1)}, bf16[256,1152]{1,0:T(8,128)(2,...) custom-call(s32[2]{0:T(128)S(1)} %pad_add_fusion.at_ref, f32[3]{0:T(128)S(1)} %pad_maximum_fusion.factors_ref, ...), custom_call_target="tpu_custom_call" | custom-call | flops 1811939328 | bytes 8257536 | tf_op jit(solution)/shard_map/across/pallas_call | solution.py:167
  40.8 2.9 %collective-permute-start.8 = (bf16[256,1152]{1,0:T(8,128)(2,1)S(1)}, bf16[256,1152]{1,0:T(8,128)(2,1)S(1)}, u32[]{:S(2)}, u32[]{:S(2)}) collective-permute-start(bf16[256,1152]{1,0:T(8,128)(2,1)S(1)} %get-tuple-element.66), channel_id=1, source_target_pairs={{0,8},{1,9},{2,10},{3,11},{4,12},{5,13},{6,14},{7,15},{8,0},{9,1},... | collective-permute-start | bytes 1769480 | tf_op jit(solution)/shard_map/core/ppermute | solution.py:55
  43.7 2.3 %far.1 = (bf16[272,1152]{1,0:T(8,128)(2,1)S(1)}, bf16[272,1152]{1,0:T(8,128)(2,1)S(1)}, bf16[256,1152]{1,0:T(8,128)(2,1)S(1)}, f32[8,256]{1,0:T(8,128)S(1)}) custom-call(s32[2]{0:T(128)S(1)} %pad_add_fusion.at_ref, f32[3]{0:T(128)S(1)} %pad_maximum_fusion.factors_ref, s32[1,2048]{1,0:T(1,128)S(1)} %copy-done, ...), custom_call_target="tpu_custom_call" | custom-call | flops 905969664 | bytes 4718592 | tf_op jit(solution)/shard_map/far/pallas_call | solution.py:167
  46.0 0.0 collective-permute-done.8.refs_6_
  46.0 2.3 %rest.1 = (bf16[256,1152]{1,0:T(8,128)(2,1)S(1)}, bf16[272,1152]{1,0:T(8,128)(2,1)S(1)}, bf16[256,1152]{1,0:T(8,128)(2,1)S(1)}, f32[8,256]{1,0:T(8,128)S(1)}) custom-call(s32[2]{0:T(128)S(1)} %pad_add_fusion.at_ref, f32[3]{0:T(128)S(1)} %pad_maximum_fusion.factors_ref, s32[1,2048]{1,0:T(1,128)S(1)} %copy-done, ...), custom_call_target="tpu_custom_call" | custom-call | flops 905969664 | bytes 5898240 | tf_op jit(solution)/shard_map/rest/pallas_call | solution.py:167
  48.3 0.1 collective-permute-start.11
  48.4 0.1 collective-permute-start.10
  48.5 2.2 %collective-permute-start.13 = (bf16[256,1152]{1,0:T(8,128)(2,1)S(1)}, bf16[256,1152]{1,0:T(8,128)(2,1)S(1)}, u32[]{:S(2)}, u32[]{:S(2)}) collective-permute-start(bf16[256,1152]{1,0:T(8,128)(2,1)S(1)} %get-tuple-element.76), channel_id=1, source_target_pairs={{0,8},{1,9},{2,10},{3,11},{4,12},{5,13},{6,14},{7,15},{8,0},{9,1},... | collective-permute-start | bytes 1769480 | tf_op jit(solution)/shard_map/core/ppermute | solution.py:55
  50.7 0.6 collective-permute-start.14
  51.4 13.9 %collective-permute-done.11.right = bf16[256,1152]{1,0:T(8,128)(2,1)S(1)} collective-permute-done((bf16[256,1152]{1,0:T(8,128)(2,1)S(1)}, bf16[256,1152]{1,0:T(8,128)(2,1)S(1)}, u32[]{:S(2)}, u32[]{:S(2)}) %collective-permute-start.11) | collective-permute-done | bytes 589856 | tf_op jit(solution)/shard_map/q/ppermute | solution.py:55
  65.2 0.1 joined.3
  65.4 0.1 collective-permute-start.15
  65.5 0.1 collective-permute-start.9
  65.6 0.0 collective-permute-done.10.right
  65.6 0.2 joined.2
  65.7 2.7 %collective-permute-start.12 = (bf16[272,1152]{1,0:T(8,128)(2,1)S(1)}, bf16[272,1152]{1,0:T(8,128)(2,1)S(1)}, u32[]{:S(2)}, u32[]{:S(2)}) collective-permute-start(bf16[272,1152]{1,0:T(8,128)(2,1)S(1)} %joined.2), channel_id=1, source_target_pairs={{0,1},{1,2},{2,3},{3,0},{4,5},{5,6},{6,7},{7,4},{8,11},{9,8},{10,9... | collective-permute-start | bytes 1880072 | tf_op jit(solution)/shard_map/x/ppermute | solution.py:55
  68.5 0.0 collective-permute-done.13
  68.5 0.0 collective-permute-done.14
  68.5 7.8 %collective-permute-done.15 = bf16[256,1152]{1,0:T(8,128)(2,1)S(1)} collective-permute-done((bf16[256,1152]{1,0:T(8,128)(2,1)S(1)}, bf16[256,1152]{1,0:T(8,128)(2,1)S(1)}, u32[]{:S(2)}, u32[]{:S(2)}) %collective-permute-start.15) | collective-permute-done | bytes 589856 | tf_op jit(solution)/shard_map/q/ppermute | solution.py:55
  76.3 1.1 %add_convert_fusion = bf16[256,1152]{1,0:T(8,128)(2,1)} fusion(bf16[256,1152]{1,0:T(8,128)(2,1)S(1)} %collective-permute-done.15, bf16[256,1152]{1,0:T(8,128)(2,1)S(1)} %collective-permute-done.14, bf16[256,1152]{1,0:T(8,128)(2,1)S(1)} %collective-permute-done.13, bf16[256,1152]{1,0:T(8,128)(2,1)S(1)} %get-tuple-element.75), kind=kLoop, calls=%fused_computation | loop fusion | flops 2359296 | bytes 2949120 | tf_op jit(solution)/shard_map/convert_element_type | solution.py:218
  77.4 5.4 %collective-permute-done.9 = bf16[272,1152]{1,0:T(8,128)(2,1)S(1)} collective-permute-done((bf16[272,1152]{1,0:T(8,128)(2,1)S(1)}, bf16[272,1152]{1,0:T(8,128)(2,1)S(1)}, u32[]{:S(2)}, u32[]{:S(2)}) %collective-permute-start.9) | collective-permute-done | bytes 626720 | tf_op jit(solution)/shard_map/x/ppermute | solution.py:55
  82.8 0.0 collective-permute-done.12
  82.8 1.0 %add_convert_fusion.1 = bf16[256,1152]{1,0:T(8,128)(2,1)} fusion(bf16[256,1152]{1,0:T(8,128)(2,1)S(1)} %get-tuple-element.74, bf16[272,1152]{1,0:T(8,128)(2,1)S(1)} %collective-permute-done.12, bf16[272,1152]{1,0:T(8,128)(2,1)S(1)} %collective-permute-done.9), kind=kLoop, calls=%fused_computation.1 | loop fusion | flops 1769472 | bytes 2359296 | tf_op jit(solution)/shard_map/convert_element_type | solution.py:218
  83.8 0.6 fusion.1
  (3 shorter events, 0.0 us)
Async XLA Ops:
  0.6 11.0 %collective-permute-start = (bf16[256,1152]{1,0:T(8,128)(2,1)}, bf16[256,1152]{1,0:T(8,128)(2,1)S(1)}, u32[]{:S(2)}, u32[]{:S(2)}) collective-permute-start(bf16[256,1152]{1,0:T(8,128)(2,1)} %refs_1_.1), channel_id=1, source_target_pairs={{0,8},{1,9},{2,10},{3,11},{4,12},{5,13},{6,14},{7,15},{8,0},{9,1},... | collective-permute-start | bytes 1769480 | tf_op jit(solution)/shard_map/core/ppermute | solution.py:55
  4.0 12.7 %collective-permute-start.2 = (bf16[256,1152]{1,0:T(8,128)(2,1)}, bf16[256,1152]{1,0:T(8,128)(2,1)S(1)}, u32[]{:S(2)}, u32[]{:S(2)}) collective-permute-start(bf16[256,1152]{1,0:T(8,128)(2,1)} %refs_1_.1), channel_id=1, source_target_pairs={{0,252},{1,253},{2,254},{3,255},{4,248},{5,249},{6,250},{7,251},{8... | collective-permute-start | bytes 1769480 | tf_op jit(solution)/shard_map/q/ppermute | solution.py:55
  4.0 12.8 %collective-permute-start.4 = (bf16[256,1152]{1,0:T(8,128)(2,1)}, bf16[256,1152]{1,0:T(8,128)(2,1)S(1)}, u32[]{:S(2)}, u32[]{:S(2)}) collective-permute-start(bf16[256,1152]{1,0:T(8,128)(2,1)} %refs_0_.1), channel_id=1, source_target_pairs={{0,1},{1,2},{2,3},{3,0},{4,5},{5,6},{6,7},{7,4},{8,11},{9,8},{10,9... | collective-permute-start | bytes 1769480 | tf_op jit(solution)/shard_map/x/ppermute | solution.py:55
  6.0 11.6 %collective-permute-start.1 = (bf16[256,1152]{1,0:T(8,128)(2,1)}, bf16[256,1152]{1,0:T(8,128)(2,1)S(1)}, u32[]{:S(2)}, u32[]{:S(2)}) collective-permute-start(bf16[256,1152]{1,0:T(8,128)(2,1)} %refs_0_.1), channel_id=1, source_target_pairs={{0,3},{1,0},{2,1},{3,2},{4,7},{5,4},{6,5},{7,6},{8,9},{9,10},{10,1... | collective-permute-start | bytes 1769480 | tf_op jit(solution)/shard_map/x/ppermute | solution.py:55
  6.0 16.7 %collective-permute-start.6 = (bf16[256,1152]{1,0:T(8,128)(2,1)}, bf16[256,1152]{1,0:T(8,128)(2,1)S(1)}, u32[]{:S(2)}, u32[]{:S(2)}) collective-permute-start(bf16[256,1152]{1,0:T(8,128)(2,1)} %refs_1_.1), channel_id=1, source_target_pairs={{0,248},{1,249},{2,250},{3,251},{4,252},{5,253},{6,254},{7,255},{8... | collective-permute-start | bytes 1769480 | tf_op jit(solution)/shard_map/q/ppermute | solution.py:55
  11.6 0.7 copy-start
  12.3 1.1 %copy-start.1 = (bf16[256,1152]{1,0:T(8,128)(2,1)S(1)}, bf16[256,1152]{1,0:T(8,128)(2,1)}, u32[]{:S(2)}) copy-start(bf16[256,1152]{1,0:T(8,128)(2,1)} %refs_0_.1) | copy-start | bytes 1769476
  13.4 1.1 %copy-start.2 = (bf16[256,1152]{1,0:T(8,128)(2,1)S(1)}, bf16[256,1152]{1,0:T(8,128)(2,1)}, u32[]{:S(2)}) copy-start(bf16[256,1152]{1,0:T(8,128)(2,1)} %refs_1_.1) | copy-start | bytes 1769476
  16.7 15.9 %collective-permute-start.3 = (bf16[256,1152]{1,0:T(8,128)(2,1)S(1)}, bf16[256,1152]{1,0:T(8,128)(2,1)S(1)}, u32[]{:S(2)}, u32[]{:S(2)}) collective-permute-start(bf16[256,1152]{1,0:T(8,128)(2,1)S(1)} %collective-permute-done.2.refs_4_.refs_2_), channel_id=1, source_target_pairs={{0,252},{1,253},{2,254},{3,255},{4,248},{5,249},{6,250},{7,251},{8... | collective-permute-start | bytes 1769480 | tf_op jit(solution)/shard_map/q/ppermute | solution.py:55
  16.8 17.3 %collective-permute-start.5 = (bf16[256,1152]{1,0:T(8,128)(2,1)S(1)}, bf16[256,1152]{1,0:T(8,128)(2,1)S(1)}, u32[]{:S(2)}, u32[]{:S(2)}) collective-permute-start(bf16[256,1152]{1,0:T(8,128)(2,1)S(1)} %collective-permute-done.4.refs_1_.refs_0_), channel_id=1, source_target_pairs={{0,1},{1,2},{2,3},{3,0},{4,5},{5,6},{6,7},{7,4},{8,11},{9,8},{10,9... | collective-permute-start | bytes 1769480 | tf_op jit(solution)/shard_map/x/ppermute | solution.py:55
  32.6 4.9 %collective-permute-start.7 = (bf16[256,1152]{1,0:T(8,128)(2,1)S(1)}, bf16[256,1152]{1,0:T(8,128)(2,1)S(1)}, u32[]{:S(2)}, u32[]{:S(2)}) collective-permute-start(bf16[256,1152]{1,0:T(8,128)(2,1)S(1)} %collective-permute-done.3.refs_2_), channel_id=1, source_target_pairs={{0,8},{1,9},{2,10},{3,11},{4,12},{5,13},{6,14},{7,15},{8,0},{9,1},... | collective-permute-start | bytes 1769480 | tf_op jit(solution)/shard_map/core/ppermute | solution.py:55
  40.8 5.2 %collective-permute-start.8 = (bf16[256,1152]{1,0:T(8,128)(2,1)S(1)}, bf16[256,1152]{1,0:T(8,128)(2,1)S(1)}, u32[]{:S(2)}, u32[]{:S(2)}) collective-permute-start(bf16[256,1152]{1,0:T(8,128)(2,1)S(1)} %get-tuple-element.66), channel_id=1, source_target_pairs={{0,8},{1,9},{2,10},{3,11},{4,12},{5,13},{6,14},{7,15},{8,0},{9,1},... | collective-permute-start | bytes 1769480 | tf_op jit(solution)/shard_map/core/ppermute | solution.py:55
  48.3 16.9 %collective-permute-start.11 = (bf16[256,1152]{1,0:T(8,128)(2,1)S(1)}, bf16[256,1152]{1,0:T(8,128)(2,1)S(1)}, u32[]{:S(2)}, u32[]{:S(2)}) collective-permute-start(bf16[256,1152]{1,0:T(8,128)(2,1)S(1)} %get-tuple-element.72), channel_id=1, source_target_pairs={{0,252},{1,253},{2,254},{3,255},{4,248},{5,249},{6,250},{7,251},{8... | collective-permute-start | bytes 1769480 | tf_op jit(solution)/shard_map/q/ppermute | solution.py:55
  48.4 17.2 %collective-permute-start.10 = (bf16[272,1152]{1,0:T(8,128)(2,1)S(1)}, bf16[272,1152]{1,0:T(8,128)(2,1)S(1)}, u32[]{:S(2)}, u32[]{:S(2)}) collective-permute-start(bf16[272,1152]{1,0:T(8,128)(2,1)S(1)} %get-tuple-element.71), channel_id=1, source_target_pairs={{0,1},{1,2},{2,3},{3,0},{4,5},{5,6},{6,7},{7,4},{8,11},{9,8},{10,9... | collective-permute-start | bytes 1880072 | tf_op jit(solution)/shard_map/x/ppermute | solution.py:55
  48.5 19.9 %collective-permute-start.13 = (bf16[256,1152]{1,0:T(8,128)(2,1)S(1)}, bf16[256,1152]{1,0:T(8,128)(2,1)S(1)}, u32[]{:S(2)}, u32[]{:S(2)}) collective-permute-start(bf16[256,1152]{1,0:T(8,128)(2,1)S(1)} %get-tuple-element.76), channel_id=1, source_target_pairs={{0,8},{1,9},{2,10},{3,11},{4,12},{5,13},{6,14},{7,15},{8,0},{9,1},... | collective-permute-start | bytes 1769480 | tf_op jit(solution)/shard_map/core/ppermute | solution.py:55
  50.7 17.8 %collective-permute-start.14 = (bf16[256,1152]{1,0:T(8,128)(2,1)S(1)}, bf16[256,1152]{1,0:T(8,128)(2,1)S(1)}, u32[]{:S(2)}, u32[]{:S(2)}) collective-permute-start(bf16[256,1152]{1,0:T(8,128)(2,1)S(1)} %get-tuple-element.77), channel_id=1, source_target_pairs={{0,248},{1,249},{2,250},{3,251},{4,252},{5,253},{6,254},{7,255},{8... | collective-permute-start | bytes 1769480 | tf_op jit(solution)/shard_map/q/ppermute | solution.py:55
  65.4 10.9 %collective-permute-start.15 = (bf16[256,1152]{1,0:T(8,128)(2,1)S(1)}, bf16[256,1152]{1,0:T(8,128)(2,1)S(1)}, u32[]{:S(2)}, u32[]{:S(2)}) collective-permute-start(bf16[256,1152]{1,0:T(8,128)(2,1)S(1)} %joined.3), channel_id=1, source_target_pairs={{0,252},{1,253},{2,254},{3,255},{4,248},{5,249},{6,250},{7,251},{8... | collective-permute-start | bytes 1769480 | tf_op jit(solution)/shard_map/q/ppermute | solution.py:55
  65.5 17.3 %collective-permute-start.9 = (bf16[272,1152]{1,0:T(8,128)(2,1)S(1)}, bf16[272,1152]{1,0:T(8,128)(2,1)S(1)}, u32[]{:S(2)}, u32[]{:S(2)}) collective-permute-start(bf16[272,1152]{1,0:T(8,128)(2,1)S(1)} %get-tuple-element.69), channel_id=1, source_target_pairs={{0,3},{1,0},{2,1},{3,2},{4,7},{5,4},{6,5},{7,6},{8,9},{9,10},{10,1... | collective-permute-start | bytes 1880072 | tf_op jit(solution)/shard_map/x/ppermute | solution.py:55
  65.7 17.0 %collective-permute-start.12 = (bf16[272,1152]{1,0:T(8,128)(2,1)S(1)}, bf16[272,1152]{1,0:T(8,128)(2,1)S(1)}, u32[]{:S(2)}, u32[]{:S(2)}) collective-permute-start(bf16[272,1152]{1,0:T(8,128)(2,1)S(1)} %joined.2), channel_id=1, source_target_pairs={{0,1},{1,2},{2,3},{3,0},{4,5},{5,6},{6,7},{7,4},{8,11},{9,8},{10,9... | collective-permute-start | bytes 1880072 | tf_op jit(solution)/shard_map/x/ppermute | solution.py:55

commit v3 on v2

v3 whole, which is shorter than its diff:
```python
import functools

import jax
import jax.numpy as jnp
from jax import lax
from jax.experimental import pallas as pl
from jax.experimental.pallas import tpu as pltpu
from jax.sharding import PartitionSpec as P

FEATURE_DIM = 1152
ROWS = 256
LOG2E = 1.4426950408889634
LN2 = 0.6931471805599453
HBM = pl.BlockSpec(memory_space=pltpu.HBM)
VMEM = pl.BlockSpec(memory_space=pltpu.VMEM)
SMEM = pl.BlockSpec(memory_space=pltpu.SMEM)
NT = (((1,), (1,)), ((), ()))
TN = (((0,), (0,)), ((), ()))
STEPS = {"i0": 0, "i1": -1, "i2": 1, "i3": 2}
IMAGES = list(STEPS)
TEXTS = ["t0", "t1", "t2", "t3", "c0", "c3"]
HOMES = {"t0": 0, "t3": 4}
AXES = ("dp", "hst")
F32 = jnp.float32
BF16 = jnp.bfloat16


def place_of(index):
    dp, hst = divmod(index, 8)
    return hst % 4, (hst // 4) * 2 + (dp // 2) % 2, dp // 4, dp % 2


def index_of(x, y, z, core):
    x, y, z = x % 4, y % 4, z % 8
    return (z * 4 + (y % 2) * 2 + core) * 8 + (y // 2) * 4 + x


def x_step(steps, x, y, z, core):
    return x + (steps if core == 0 else -steps), y, z, core


def q_step(steps, x, y, z, core):
    in_plane = y % 2 != core
    if not in_plane:
        z = z - 1 if core == 0 else z + 1
    return x, y + (steps if in_plane else -steps), z, 1 - core


def core_step(x, y, z, core):
    return x, y, z, 1 - core


def moved(value, step):
    pairs = [(i, index_of(*step(*place_of(i)))) for i in range(256)]
    return lax.ppermute(value, AXES, pairs)


def pair_terms(product, factors, positive):
    z = product * factors[0] + factors[1]
    if positive is not None:
        z = jnp.where(positive, -z, z)
    e = jnp.exp2(-jnp.abs(z))
    u = 1.0 + e
    log_u = jnp.where(e < 2.0**-8, LOG2E * e * (1.0 - 0.5 * e), jnp.log2(u))
    softplus = jnp.maximum(z, 0.0) + log_u
    scale = factors[2]
    coefficient = jnp.where(z >= 0.0, scale, scale * e) * pltpu.reciprocal(u, approx=True)
    if positive is not None:
        coefficient = jnp.where(positive, -coefficient, coefficient)
    return coefficient, softplus


def pairs_kernel(plan, at_ref, factors_ref, slot_ref, *refs):
    pairs, names, old_names, known, n_loss, grads, fetched, framed = plan
    refs = list(refs)

    def take(keys):
        return {key: refs.pop(0) for key in keys}

    blocks, old = take(names), take(old_names)
    known_refs, loss_refs = take(range(len(known))), take(range(n_loss))
    new, copies = take(list(grads)), take(fetched)
    loss_out, coef = refs.pop(0), refs.pop(0)
    if fetched:
        sources = {**blocks, "slot": slot_ref}
        moves = [
            pltpu.make_async_copy(sources[name], copies[name], refs[0].at[n])
            for n, name in enumerate(fetched)
        ]
        for move in moves:
            move.start()
        for move in moves:
            move.wait()
        blocks = {**blocks, **copies}
        slot_ref = copies["slot"]
    images = [n for n in IMAGES if any(n == i for i, _ in pairs)]
    texts = [n for n in TEXTS if any(n == t for _, t in pairs)]
    factors = [factors_ref[n] for n in range(3)]
    at = at_ref[0]
    columns = lax.broadcasted_iota(jnp.int32, (ROWS, ROWS), 1)
    sums, wanted, spots = {}, {}, {}

    def placed(ref, rows, cols):
        for i in rows:
            for t in cols:
                at_row, at_col = rows.index(i) * ROWS, cols.index(t) * ROWS
                spots[i, t] = ref.at[pl.ds(at_row, ROWS), pl.ds(at_col, ROWS)]

    for n, (rows, cols) in enumerate(known):
        placed(known_refs[n], rows, cols)
    placed(coef, images, texts)

    def place_wanted(i):
        if i not in wanted:
            place = ((at & 4) + ((at + STEPS[i] * at_ref[1]) & 3)) * ROWS
            row = slot_ref[:, pl.ds(pl.multiple_of(place, ROWS), ROWS)]
            wanted[i] = jnp.broadcast_to(row, (128, ROWS)).T[:, :1]
        return wanted[i]

    for i, t in pairs:
        product = lax.dot_general(
            blocks[i][...], blocks[t][...], NT, preferred_element_type=F32
        )
        positive = None
        if t in HOMES:
            positive = columns == place_wanted(i) - (at ^ HOMES[t]) * ROWS
        coefficient, softplus = pair_terms(product, factors, positive)
        spots[i, t][...] = coefficient.astype(BF16)
        part = softplus[:, :128] + softplus[:, 128:]
        sums[i] = part if i not in sums else sums[i] + part

    values = {}
    for n, i in enumerate(IMAGES):
        row = pl.ds(n, 1)
        value = jnp.zeros((1, ROWS), F32)
        if i in sums:
            value = jnp.sum(sums[i].T, axis=0, keepdims=True)
        for ref in loss_refs.values():
            value = value + ref[row, :]
        loss_out[row, :] = values[i] = value

    for name, partners in grads.items():
        others = jnp.concatenate([blocks[p][...] for p in partners])
        if name in IMAGES:
            weights = jnp.concatenate([spots[name, p][...] for p in partners], axis=1)
            total = jnp.dot(weights, others, preferred_element_type=F32)
        else:
            weights = jnp.concatenate([spots[p, name][...] for p in partners])
            total = lax.dot_general(weights, others, TN, preferred_element_type=F32)
        if name in old:
            total = total + old[name][...].astype(F32)
        if name == "t3" and "more" in old:
            total = total + old["more"][...].astype(F32)
        new[name][pl.ds(0, ROWS), :] = total.astype(BF16)
        if name in framed:
            at_row = lax.broadcasted_iota(jnp.int32, (16, ROWS), 0)
            large = values[name].astype(BF16).astype(F32)
            small = values[name] - large
            both = jnp.where(at_row == 0, large, jnp.where(at_row == 1, small, 0.0))
            new[name][pl.ds(ROWS, 16), :] = jnp.zeros((16, FEATURE_DIM), BF16)
            new[name][pl.ds(ROWS, 16), pl.ds(0, ROWS)] = both.astype(BF16)


def pair_call(
    name, common, values, pairs, grads, old=None, known=(), losses=(), fetched=(), framed=()
):
    old = old or {}
    images = [n for n in IMAGES if any(n == i for i, _ in pairs)]
    texts = [n for n in TEXTS if any(n == t for _, t in pairs)]
    partners = [p for ps in grads.values() for p in ps]
    names = [n for n in [*IMAGES, *TEXTS] if n in images + texts + partners]
    old_names = [n for n in [*grads, "more"] if n in old]
    known_at = [(rows, cols) for rows, cols, _ in known]
    plan = (pairs, names, old_names, known_at, len(losses), grads, fetched, framed)
    block_specs = [HBM if n in fetched else VMEM for n in names]
    operands = [
        *(values[n] for n in names), *(old[n] for n in old_names),
        *(ref for _, _, ref in known), *losses,
    ]
    rows = [ROWS + 16 if n in framed else ROWS for n in grads]
    shapes = [jax.ShapeDtypeStruct((r, FEATURE_DIM), BF16) for r in rows]
    shapes += [
        jax.ShapeDtypeStruct(common[2].shape, jnp.int32)
        if n == "slot"
        else jax.ShapeDtypeStruct((ROWS, FEATURE_DIM), BF16)
        for n in fetched
    ]
    shapes += [
        jax.ShapeDtypeStruct((8, ROWS), F32),
        jax.ShapeDtypeStruct((max(len(images), 1) * ROWS, max(len(texts), 1) * ROWS), BF16),
    ]
    out = pl.pallas_call(
        functools.partial(pairs_kernel, plan),
        name=name,
        out_shape=shapes,
        in_specs=[SMEM, SMEM, HBM if fetched else VMEM, *block_specs]
        + [VMEM] * (len(operands) - len(names)),
        out_specs=[VMEM] * len(shapes),
        scratch_shapes=[pltpu.SemaphoreType.DMA((len(fetched),))] if fetched else [],
        compiler_params=pltpu.CompilerParams(vmem_limit_bytes=24 << 20),
        cost_estimate=pl.CostEstimate(
            flops=2 * (len(pairs) + len(partners)) * ROWS * ROWS * FEATURE_DIM,
            bytes_accessed=2 * ROWS * FEATURE_DIM * (len(operands) + len(shapes)),
            transcendentals=0,
        ),
    )(*common, *operands)
    new = dict(zip([*grads, *(f"{n} block" for n in fetched)], out))
    return {**old, **new}, out[-2], (images, texts, out[-1])


def joined_kernel(left, right, out):
    rows = pl.ds(0, ROWS)
    out[rows, :] = (left[rows, :].astype(F32) + right[rows, :].astype(F32)).astype(BF16)
    if out.shape[0] > ROWS:
        rows = pl.ds(ROWS, 16)
        both = left[rows, :].astype(F32) + right[rows, :].astype(F32)
        value = both[0:1] + both[1:2]
        at_row = lax.broadcasted_iota(jnp.int32, both.shape, 0)
        large = value.astype(BF16).astype(F32)
        out[rows, :] = jnp.where(
            at_row == 0, large, jnp.where(at_row == 1, value - large, 0.0)
        ).astype(BF16)


def joined(left, right):
    return pl.pallas_call(
        joined_kernel,
        name="joined",
        out_shape=jax.ShapeDtypeStruct(left.shape, BF16),
        in_specs=[VMEM, VMEM],
        out_specs=VMEM,
        compiler_params=pltpu.CompilerParams(vmem_limit_bytes=16 << 20),
        cost_estimate=pl.CostEstimate(
            flops=ROWS * FEATURE_DIM, bytes_accessed=6 * ROWS * FEATURE_DIM, transcendentals=0
        ),
    )(left, right)


def summed(*terms):
    total = terms[0][:ROWS].astype(F32)
    for term in terms[1:]:
        total = total + term[:ROWS].astype(F32)
    return total.astype(BF16)


def tied(value, *others):
    return lax.optimization_barrier((value, *others))[0]


def on_device(images, texts, slot, heat, offset):
    scale = heat[0] / FEATURE_DIM
    factors = jnp.stack([scale * LOG2E, offset[0] * LOG2E, scale])
    way = 1 - 2 * (lax.axis_index("dp") & 1)
    at = jnp.stack([lax.axis_index("hst"), way]).astype(jnp.int32)
    common = (at, factors, slot)

    def xs(value, n):
        with jax.named_scope("x"):
            return moved(value, functools.partial(x_step, n))

    def qs(value, n):
        with jax.named_scope("q"):
            return moved(value, functools.partial(q_step, n))

    def across(value):
        with jax.named_scope("core"):
            return moved(value, core_step)

    v = {"i0": images, "t0": texts}
    v["t1"], v["i1"] = qs(texts, 1), xs(images, 1)
    v["t2"], v["i2"] = qs(texts, -1), xs(images, -1)
    v["c0"] = across(texts)
    near = ("t1", "t2", "t0", "c0")
    g, loss, _ = pair_call(
        "own", common, v, [("i0", "t0"), ("i0", "c0")],
        {"i0": ("t0", "c0"), "t0": ("i0",), "c0": ("i0",)}, fetched=("i0", "t0", "slot"),
    )
    v = {**v, "i0": g["i0 block"], "t0": g["t0 block"]}
    call = functools.partial(pair_call, common=(at, factors, g["slot block"]))
    v["t3"] = qs(tied(v["t1"], loss), 1)
    v["i3"] = xs(tied(v["i1"], loss), 1)
    g, loss, _ = call(
        "near", values=v, old=g, losses=(loss,),
        pairs=[(i, t) for i in ("i1", "i2") for t in near] + [("i0", "t1"), ("i0", "t2")],
        grads={
            "i0": ("t1", "t2"), "i1": near, "i2": near, "t0": ("i1", "i2"),
            "c0": ("i1", "i2"), "t1": ("i0", "i1", "i2"), "t2": ("i0", "i1", "i2"),
        },
    )
    v["c3"] = across(tied(v["t3"], loss))
    g, loss, from_third = call(
        "third", values=v, old=g, losses=(loss,), pairs=[("i3", t) for t in near],
        grads={"t1": ("i3",), "i3": near},
    )
    g, loss, from_across = call(
        "across", values=v, old=g, losses=(loss,), pairs=[(i, "c3") for i in IMAGES],
        grads={"c3": IMAGES},
    )
    far_core = across(g["c3"])
    g, loss, from_far = call(
        "far", values=v, old=g, losses=(loss,), pairs=[("i3", "t3"), ("i1", "t3")],
        known=(from_across,), grads={"i3": ("c3", "t3"), "i1": ("c3", "t3")},
        framed=("i1", "i3"),
    )
    image_far = xs(g["i3"], 1)
    image_next = xs(g["i1"], -1)
    g, loss, from_rest = call(
        "rest", values=v, old={**g, "more": far_core}, losses=(loss,),
        pairs=[("i0", "t3"), ("i2", "t3")], known=(from_far,), grads={"t3": IMAGES},
    )
    text_far = qs(g["t3"], 1)
    g, _, _ = call(
        "wrap", values=v, old=g, losses=(loss,), pairs=[],
        known=(from_third, from_across, from_rest),
        grads={
            "t2": ("i3",), "c0": ("i3",), "t0": ("i3",), "i2": ("c3", "t3"), "i0": ("c3", "t3")
        },
        framed=("i2",),
    )
    from_core = across(g["c0"])
    from_next = qs(tied(g["t1"], g["c0"]), -1)
    text_prev = qs(joined(g["t2"], text_far), 1)
    image_prev = xs(joined(g["i2"], tied(image_far, text_far, image_next)), 1)
    row_loss = loss[0]
    for s in (image_next, image_prev):
        row_loss = row_loss + s[ROWS, :ROWS].astype(F32) + s[ROWS + 1, :ROWS].astype(F32)
    grad_image = summed(g["i0"], image_next, image_prev)
    grad_text = summed(g["t0"], from_core, from_next, text_prev)
    return row_loss * (LN2 / 6144), grad_image, grad_text


def solution(mesh):
    in_specs = (P(AXES, None), P(AXES, None), P("dp", None), P(), P())
    out_specs = (P(AXES), P(AXES, None), P(AXES, None))
    return jax.shard_map(
        on_device, mesh=mesh, in_specs=in_specs, out_specs=out_specs, check_vma=False
    )
```

time: 84.6 us -> 76.4 us (0.903)
  waiting for transfers between devices: 35.5 us -> 25.3 us
  Pallas kernels: 21 us -> 22.3 us
    ppermute x16, waiting for transfers between devices: 35.5 us -> 25.3 us  [moved(): return lax.ppermute(value, AXES, pairs)]
    pallas_call x6 -> x7, Pallas kernels: 20.7 us -> 22 us  [pair_call(): pl.pallas_call(functools.partial(pairs_kernel, plan), name=name, out_shap...]
  transfers between devices with their start and end apart: 16 -> 16, of which waited for: 6 -> 8; matrix products, arithmetic and copies ran while one was open for 1% -> 2% of each run, Pallas kernels for 18% -> 23%
where the time goes in v3:
time: 76.4 us; the launch traced here: 76.2 us
  waiting for transfers between devices  25.3 us (33%)
  Pallas kernels  22.3 us (29%)
  starting transfers between devices  20.9 us (27%)
  other arithmetic  2.87 us (4%)
  local copies, waits for them, and re-layouts  2.83 us (4%)
  between operations  2.05 us (3%)
    ppermute x16, waiting for transfers between devices, moved(): return lax.ppermute(value, AXES, pairs)  25.3 us
    pallas_call x7, Pallas kernels, pair_call(): pl.pallas_call(functools.partial(pairs_kernel, plan), name=name, out_shap...  22 us
    ppermute x16, starting transfers between devices, moved(): return lax.ppermute(value, AXES, pairs)  20.9 us
    unnamed x6, local copies, waits for them, and re-layouts  2.83 us
    convert_element_type x2, other arithmetic, summed(): return total.astype(BF16)  2.14 us
  transfers between devices with their start and end apart: 16, of which 8 were waited for; matrix products, arithmetic and copies ran while one was open for 2% of the time, Pallas kernels for 23%

profile of v3, /device:TPU:1, one launch (start us, length us, event | category | flops | bytes accessed | tf_op | source)
XLA Modules:
  0.0 76.2 jit_solution(11418046800447381070)
XLA Ops:
  0.6 3.3 %collective-permute-start = (bf16[256,1152]{1,0:T(8,128)(2,1)}, bf16[256,1152]{1,0:T(8,128)(2,1)S(1)}, u32[]{:S(2)}, u32[]{:S(2)}) collective-permute-start(bf16[256,1152]{1,0:T(8,128)(2,1)} %refs_1_.1), channel_id=1, source_target_pairs={{0,8},{1,9},{2,10},{3,11},{4,12},{5,13},{6,14},{7,15},{8,0},{9,1},... | collective-permute-start | bytes 1769480 | tf_op jit(solution)/shard_map/core/ppermute | solution.py:55
  4.0 0.0 collective-permute-start.4
  4.0 2.0 %collective-permute-start.1 = (bf16[256,1152]{1,0:T(8,128)(2,1)}, bf16[256,1152]{1,0:T(8,128)(2,1)S(1)}, u32[]{:S(2)}, u32[]{:S(2)}) collective-permute-start(bf16[256,1152]{1,0:T(8,128)(2,1)} %refs_0_.1), channel_id=1, source_target_pairs={{0,1},{1,2},{2,3},{3,0},{4,5},{5,6},{6,7},{7,4},{8,11},{9,8},{10,9... | collective-permute-start | bytes 1769480 | tf_op jit(solution)/shard_map/x/ppermute | solution.py:55
  6.0 0.0 collective-permute-start.2
  6.0 4.2 %collective-permute-start.6 = (bf16[256,1152]{1,0:T(8,128)(2,1)}, bf16[256,1152]{1,0:T(8,128)(2,1)S(1)}, u32[]{:S(2)}, u32[]{:S(2)}) collective-permute-start(bf16[256,1152]{1,0:T(8,128)(2,1)} %refs_1_.1), channel_id=1, source_target_pairs={{0,248},{1,249},{2,250},{3,251},{4,252},{5,253},{6,254},{7,255},{8... | collective-permute-start | bytes 1769480 | tf_op jit(solution)/shard_map/q/ppermute | solution.py:55
  11.4 0.1 pad_add_fusion.at_ref
  11.5 0.1 pad_maximum_fusion.factors_ref
  11.6 0.0 collective-permute-done.refs_2_.refs_6_.refs_4_
  11.6 1.1 %copy-done = bf16[256,1152]{1,0:T(8,128)(2,1)S(1)} copy-done((bf16[256,1152]{1,0:T(8,128)(2,1)S(1)}, bf16[256,1152]{1,0:T(8,128)(2,1)}, u32[]{:S(2)}) %copy-start) | copy-done | bytes 589848
  12.7 1.1 %copy-done.1 = bf16[256,1152]{1,0:T(8,128)(2,1)S(1)} copy-done((bf16[256,1152]{1,0:T(8,128)(2,1)S(1)}, bf16[256,1152]{1,0:T(8,128)(2,1)}, u32[]{:S(2)}) %copy-start.1) | copy-done | bytes 589848
  13.7 0.7 copy-done.2
  14.4 2.5 %own.1 = (bf16[256,1152]{1,0:T(8,128)(2,1)S(1)}, bf16[256,1152]{1,0:T(8,128)(2,1)S(1)}, bf16[256,1152]{1,0:T(8,128)(2,1)S(1)}, bf16[256,1152]{1,0:T(8,128)(2,1)S...) custom-call(s32[2]{0:T(128)S(1)} %pad_add_fusion.at_ref, ...), custom_call_target="tpu_custom_call" | custom-call | flops 905969664 | bytes 6488064 | tf_op jit(solution)/shard_map/own/pallas_call | solution.py:192
  17.0 0.0 collective-permute-done.4.refs_4_.refs_2_
  17.0 0.1 collective-permute-start.5
  17.1 0.0 collective-permute-done.1.refs_1_.refs_0_
  17.1 0.3 collective-permute-start.3
  17.3 0.2 collective-permute-done.2.refs_2_
  17.6 5.2 %collective-permute-done.6.refs_5_.refs_3_ = bf16[256,1152]{1,0:T(8,128)(2,1)S(1)} collective-permute-done((bf16[256,1152]{1,0:T(8,128)(2,1)}, bf16[256,1152]{1,0:T(8,128)(2,1)S(1)}, u32[]{:S(2)}, u32[]{:S(2)}) %collective-permute-start.6) | collective-permute-done | bytes 589856 | tf_op jit(solution)/shard_map/q/ppermute | solution.py:55
  22.7 7.2 %near.1 = (bf16[256,1152]{1,0:T(8,128)(2,1)S(1)}, bf16[256,1152]{1,0:T(8,128)(2,1)S(1)}, bf16[256,1152]{1,0:T(8,128)(2,1)S(1)}, bf16[256,1152]{1,0:T(8,128)(2,1)...) custom-call(s32[2]{0:T(128)S(1)} %pad_add_fusion.at_ref, ...), custom_call_target="tpu_custom_call" | custom-call | flops 4529848320 | bytes 11796480 | tf_op jit(solution)/shard_map/near/pallas_call | solution.py:192
  29.9 2.7 %collective-permute-done.5.refs_2_.refs_4_.refs_1_ = bf16[256,1152]{1,0:T(8,128)(2,1)S(1)} collective-permute-done((bf16[256,1152]{1,0:T(8,128)(2,1)S(1)}, bf16[256,1152]{1,0:T(8,128)(2,1)S(1)}, u32[]{:S(2)}, u32[]{:S(2)}) %collective-permute-start.5) | collective-permute-done | bytes 589856 | tf_op jit(solution)/shard_map/q/ppermute | solution.py:55
  32.6 1.4 %collective-permute-start.7 = (bf16[256,1152]{1,0:T(8,128)(2,1)S(1)}, bf16[256,1152]{1,0:T(8,128)(2,1)S(1)}, u32[]{:S(2)}, u32[]{:S(2)}) collective-permute-start(bf16[256,1152]{1,0:T(8,128)(2,1)S(1)} %collective-permute-done.5.refs_2_.refs_4_.refs_1_), channel_id=1, source_target_pairs={{0,8},{1,9},{2,10},{3,11},{4,12},{5,13},{6,14},{7,15},{8,0},{9,1},... | collective-permute-start | bytes 1769480 | tf_op jit(solution)/shard_map/core/ppermute | solution.py:55
  34.0 0.0 collective-permute-done.3.refs_0_.refs_3_.refs_1_
  34.0 2.7 %third.1 = (bf16[256,1152]{1,0:T(8,128)(2,1)S(1)}, bf16[256,1152]{1,0:T(8,128)(2,1)S(1)}, f32[8,256]{1,0:T(8,128)S(1)}, bf16[256,1024]{1,0:T(8,128)(2,1)S(1)}) custom-call(s32[2]{0:T(128)S(1)} %pad_add_fusion.at_ref, f32[3]{0:T(128)S(1)} %pad_maximum_fusion.factors_ref, s32[1,2048]{1,0:T(1,128)S(1)} %get-tuple-element.42.slot_ref, ...), custom_call_target="tpu_custom_call" | custom-call | flops 1358954496 | bytes 6488064 | tf_op jit(solution)/shard_map/third/pallas_call | solution.py:192
  36.7 0.0 collective-permute-done.7.refs_4_.refs_3_.refs_2_
  36.7 2.5 %across.1 = (bf16[256,1152]{1,0:T(8,128)(2,1)S(1)}, f32[8,256]{1,0:T(8,128)S(1)}, bf16[1024,256]{1,0:T(8,128)(2,1)S(1)}) custom-call(s32[2]{0:T(128)S(1)} %pad_add_fusion.at_ref, f32[3]{0:T(128)S(1)} %pad_maximum_fusion.factors_ref, s32[1,2048]{1,0:T(1,128)S(1)} %get-tuple-element.42.slot_ref, bf16[256,1152]{1,0:T(8,128)(2,1)S(1)} %get-tuple-element.43.refs_0_, ...), custom_call_target="tpu_custom_call" | custom-call | flops 1207959552 | bytes 5308416 | tf_op jit(solution)/shard_map/across/pallas_call | solution.py:192
  39.3 3.2 %collective-permute-start.8 = (bf16[256,1152]{1,0:T(8,128)(2,1)S(1)}, bf16[256,1152]{1,0:T(8,128)(2,1)S(1)}, u32[]{:S(2)}, u32[]{:S(2)}) collective-permute-start(bf16[256,1152]{1,0:T(8,128)(2,1)S(1)} %get-tuple-element.55), channel_id=1, source_target_pairs={{0,8},{1,9},{2,10},{3,11},{4,12},{5,13},{6,14},{7,15},{8,0},{9,1},... | collective-permute-start | bytes 1769480 | tf_op jit(solution)/shard_map/core/ppermute | solution.py:55
  42.5 2.2 %far.1 = (bf16[272,1152]{1,0:T(8,128)(2,1)S(1)}, bf16[272,1152]{1,0:T(8,128)(2,1)S(1)}, f32[8,256]{1,0:T(8,128)S(1)}, bf16[512,256]{1,0:T(8,128)(2,1)S(1)}) custom-call(s32[2]{0:T(128)S(1)} %pad_add_fusion.at_ref, f32[3]{0:T(128)S(1)} %pad_maximum_fusion.factors_ref, s32[1,2048]{1,0:T(1,128)S(1)} %get-tuple-element.42.slot_ref, ...), custom_call_target="tpu_custom_call" | custom-call | flops 905969664 | bytes 7077888 | tf_op jit(solution)/shard_map/far/pallas_call | solution.py:192
  44.7 0.0 collective-permute-done.8.refs_5_.refs_8_
  44.7 2.4 %rest.1 = (bf16[256,1152]{1,0:T(8,128)(2,1)S(1)}, f32[8,256]{1,0:T(8,128)S(1)}, bf16[512,256]{1,0:T(8,128)(2,1)S(1)}) custom-call(s32[2]{0:T(128)S(1)} %pad_add_fusion.at_ref, f32[3]{0:T(128)S(1)} %pad_maximum_fusion.factors_ref, s32[1,2048]{1,0:T(1,128)S(1)} %get-tuple-element.42.slot_ref, bf16[256,1152]{1,0:T(8,128)(2,1)S(1)} %get-tuple-element.43.refs_0_, ...), custom_call_target="tpu_custom_call" | custom-call | flops 905969664 | bytes 6488064 | tf_op jit(solution)/shard_map/rest/pallas_call | solution.py:192
  47.0 0.1 collective-permute-start.11
  47.1 0.1 collective-permute-start.10
  47.3 1.4 %collective-permute-start.9 = (bf16[272,1152]{1,0:T(8,128)(2,1)S(1)}, bf16[272,1152]{1,0:T(8,128)(2,1)S(1)}, u32[]{:S(2)}, u32[]{:S(2)}) collective-permute-start(bf16[272,1152]{1,0:T(8,128)(2,1)S(1)} %get-tuple-element.63), channel_id=1, source_target_pairs={{0,3},{1,0},{2,1},{3,2},{4,7},{5,4},{6,5},{7,6},{8,9},{9,10},{10,1... | collective-permute-start | bytes 1880072 | tf_op jit(solution)/shard_map/x/ppermute | solution.py:55
  48.7 2.5 %wrap.1 = (bf16[256,1152]{1,0:T(8,128)(2,1)S(1)}, bf16[256,1152]{1,0:T(8,128)(2,1)S(1)}, bf16[256,1152]{1,0:T(8,128)(2,1)S(1)}, bf16[272,1152]{1,0:T(8,128)(2,1)...) custom-call(s32[2]{0:T(128)S(1)} %pad_add_fusion.at_ref, ...), custom_call_target="tpu_custom_call" | custom-call | flops 1056964608 | bytes 11796480 | tf_op jit(solution)/shard_map/wrap/pallas_call | solution.py:192
  51.2 3.7 %collective-permute-start.13 = (bf16[256,1152]{1,0:T(8,128)(2,1)S(1)}, bf16[256,1152]{1,0:T(8,128)(2,1)S(1)}, u32[]{:S(2)}, u32[]{:S(2)}) collective-permute-start(bf16[256,1152]{1,0:T(8,128)(2,1)S(1)} %get-tuple-element.77), channel_id=1, source_target_pairs={{0,8},{1,9},{2,10},{3,11},{4,12},{5,13},{6,14},{7,15},{8,0},{9,1},... | collective-permute-start | bytes 1769480 | tf_op jit(solution)/shard_map/core/ppermute | solution.py:55
  54.9 0.9 %collective-permute-start.14 = (bf16[256,1152]{1,0:T(8,128)(2,1)S(1)}, bf16[256,1152]{1,0:T(8,128)(2,1)S(1)}, u32[]{:S(2)}, u32[]{:S(2)}) collective-permute-start(bf16[256,1152]{1,0:T(8,128)(2,1)S(1)} %get-tuple-element.79), channel_id=1, source_target_pairs={{0,248},{1,249},{2,250},{3,251},{4,252},{5,253},{6,254},{7,255},{8... | collective-permute-start | bytes 1769480 | tf_op jit(solution)/shard_map/q/ppermute | solution.py:55
  55.8 2.1 %collective-permute-done.11.right = bf16[256,1152]{1,0:T(8,128)(2,1)S(1)} collective-permute-done((bf16[256,1152]{1,0:T(8,128)(2,1)S(1)}, bf16[256,1152]{1,0:T(8,128)(2,1)S(1)}, u32[]{:S(2)}, u32[]{:S(2)}) %collective-permute-start.11) | collective-permute-done | bytes 589856 | tf_op jit(solution)/shard_map/q/ppermute | solution.py:55
  57.9 0.1 joined.3
  58.1 0.1 collective-permute-start.15
  58.2 2.4 %collective-permute-done.10.right = bf16[272,1152]{1,0:T(8,128)(2,1)S(1)} collective-permute-done((bf16[272,1152]{1,0:T(8,128)(2,1)S(1)}, bf16[272,1152]{1,0:T(8,128)(2,1)S(1)}, u32[]{:S(2)}, u32[]{:S(2)}) %collective-permute-start.10) | collective-permute-done | bytes 626720 | tf_op jit(solution)/shard_map/x/ppermute | solution.py:55
  60.6 1.7 %collective-permute-done.9 = bf16[272,1152]{1,0:T(8,128)(2,1)S(1)} collective-permute-done((bf16[272,1152]{1,0:T(8,128)(2,1)S(1)}, bf16[272,1152]{1,0:T(8,128)(2,1)S(1)}, u32[]{:S(2)}, u32[]{:S(2)}) %collective-permute-start.9) | collective-permute-done | bytes 626720 | tf_op jit(solution)/shard_map/x/ppermute | solution.py:55
  62.2 0.2 joined.2
  62.4 0.1 collective-permute-start.12
  62.5 6.5 %collective-permute-done.14 = bf16[256,1152]{1,0:T(8,128)(2,1)S(1)} collective-permute-done((bf16[256,1152]{1,0:T(8,128)(2,1)S(1)}, bf16[256,1152]{1,0:T(8,128)(2,1)S(1)}, u32[]{:S(2)}, u32[]{:S(2)}) %collective-permute-start.14) | collective-permute-done | bytes 589856 | tf_op jit(solution)/shard_map/q/ppermute | solution.py:55
  68.9 0.0 collective-permute-done.13
  69.0 4.5 %collective-permute-done.15 = bf16[256,1152]{1,0:T(8,128)(2,1)S(1)} collective-permute-done((bf16[256,1152]{1,0:T(8,128)(2,1)S(1)}, bf16[256,1152]{1,0:T(8,128)(2,1)S(1)}, u32[]{:S(2)}, u32[]{:S(2)}) %collective-permute-start.15) | collective-permute-done | bytes 589856 | tf_op jit(solution)/shard_map/q/ppermute | solution.py:55
  73.5 1.1 %add_convert_fusion = bf16[256,1152]{1,0:T(8,128)(2,1)} fusion(bf16[256,1152]{1,0:T(8,128)(2,1)S(1)} %collective-permute-done.15, bf16[256,1152]{1,0:T(8,128)(2,1)S(1)} %collective-permute-done.14, bf16[256,1152]{1,0:T(8,128)(2,1)S(1)} %collective-permute-done.13, bf16[256,1152]{1,0:T(8,128)(2,1)S(1)} %get-tuple-element.76), kind=kLoop, calls=%fused_computation | loop fusion | flops 2359296 | bytes 2949120 | tf_op jit(solution)/shard_map/convert_element_type | solution.py:243
  74.6 0.6 fusion.1
  75.1 1.0 %add_convert_fusion.1 = bf16[256,1152]{1,0:T(8,128)(2,1)} fusion(bf16[256,1152]{1,0:T(8,128)(2,1)S(1)} %get-tuple-element.75, bf16[272,1152]{1,0:T(8,128)(2,1)S(1)} %collective-permute-done.12, bf16[272,1152]{1,0:T(8,128)(2,1)S(1)} %collective-permute-done.9), kind=kLoop, calls=%fused_computation.1 | loop fusion | flops 1769472 | bytes 2359296 | tf_op jit(solution)/shard_map/convert_element_type | solution.py:243
  (4 shorter events, 0.0 us)
Async XLA Ops:
  0.6 11.0 %collective-permute-start = (bf16[256,1152]{1,0:T(8,128)(2,1)}, bf16[256,1152]{1,0:T(8,128)(2,1)S(1)}, u32[]{:S(2)}, u32[]{:S(2)}) collective-permute-start(bf16[256,1152]{1,0:T(8,128)(2,1)} %refs_1_.1), channel_id=1, source_target_pairs={{0,8},{1,9},{2,10},{3,11},{4,12},{5,13},{6,14},{7,15},{8,0},{9,1},... | collective-permute-start | bytes 1769480 | tf_op jit(solution)/shard_map/core/ppermute | solution.py:55
  4.0 13.0 %collective-permute-start.4 = (bf16[256,1152]{1,0:T(8,128)(2,1)}, bf16[256,1152]{1,0:T(8,128)(2,1)S(1)}, u32[]{:S(2)}, u32[]{:S(2)}) collective-permute-start(bf16[256,1152]{1,0:T(8,128)(2,1)} %refs_1_.1), channel_id=1, source_target_pairs={{0,252},{1,253},{2,254},{3,255},{4,248},{5,249},{6,250},{7,251},{8... | collective-permute-start | bytes 1769480 | tf_op jit(solution)/shard_map/q/ppermute | solution.py:55
  4.0 13.1 %collective-permute-start.1 = (bf16[256,1152]{1,0:T(8,128)(2,1)}, bf16[256,1152]{1,0:T(8,128)(2,1)S(1)}, u32[]{:S(2)}, u32[]{:S(2)}) collective-permute-start(bf16[256,1152]{1,0:T(8,128)(2,1)} %refs_0_.1), channel_id=1, source_target_pairs={{0,1},{1,2},{2,3},{3,0},{4,5},{5,6},{6,7},{7,4},{8,11},{9,8},{10,9... | collective-permute-start | bytes 1769480 | tf_op jit(solution)/shard_map/x/ppermute | solution.py:55
  6.0 11.6 %collective-permute-start.2 = (bf16[256,1152]{1,0:T(8,128)(2,1)}, bf16[256,1152]{1,0:T(8,128)(2,1)S(1)}, u32[]{:S(2)}, u32[]{:S(2)}) collective-permute-start(bf16[256,1152]{1,0:T(8,128)(2,1)} %refs_0_.1), channel_id=1, source_target_pairs={{0,3},{1,0},{2,1},{3,2},{4,7},{5,4},{6,5},{7,6},{8,9},{9,10},{10,1... | collective-permute-start | bytes 1769480 | tf_op jit(solution)/shard_map/x/ppermute | solution.py:55
  6.0 16.7 %collective-permute-start.6 = (bf16[256,1152]{1,0:T(8,128)(2,1)}, bf16[256,1152]{1,0:T(8,128)(2,1)S(1)}, u32[]{:S(2)}, u32[]{:S(2)}) collective-permute-start(bf16[256,1152]{1,0:T(8,128)(2,1)} %refs_1_.1), channel_id=1, source_target_pairs={{0,248},{1,249},{2,250},{3,251},{4,252},{5,253},{6,254},{7,255},{8... | collective-permute-start | bytes 1769480 | tf_op jit(solution)/shard_map/q/ppermute | solution.py:55
  11.6 1.1 %copy-start = (bf16[256,1152]{1,0:T(8,128)(2,1)S(1)}, bf16[256,1152]{1,0:T(8,128)(2,1)}, u32[]{:S(2)}) copy-start(bf16[256,1152]{1,0:T(8,128)(2,1)} %refs_0_.1) | copy-start | bytes 1769476
  12.7 1.1 %copy-start.1 = (bf16[256,1152]{1,0:T(8,128)(2,1)S(1)}, bf16[256,1152]{1,0:T(8,128)(2,1)}, u32[]{:S(2)}) copy-start(bf16[256,1152]{1,0:T(8,128)(2,1)} %refs_1_.1) | copy-start | bytes 1769476
  13.7 0.7 copy-start.2
  17.0 15.7 %collective-permute-start.5 = (bf16[256,1152]{1,0:T(8,128)(2,1)S(1)}, bf16[256,1152]{1,0:T(8,128)(2,1)S(1)}, u32[]{:S(2)}, u32[]{:S(2)}) collective-permute-start(bf16[256,1152]{1,0:T(8,128)(2,1)S(1)} %collective-permute-done.4.refs_4_.refs_2_), channel_id=1, source_target_pairs={{0,252},{1,253},{2,254},{3,255},{4,248},{5,249},{6,250},{7,251},{8... | collective-permute-start | bytes 1769480 | tf_op jit(solution)/shard_map/q/ppermute | solution.py:55
  17.1 17.0 %collective-permute-start.3 = (bf16[256,1152]{1,0:T(8,128)(2,1)S(1)}, bf16[256,1152]{1,0:T(8,128)(2,1)S(1)}, u32[]{:S(2)}, u32[]{:S(2)}) collective-permute-start(bf16[256,1152]{1,0:T(8,128)(2,1)S(1)} %collective-permute-done.1.refs_1_.refs_0_), channel_id=1, source_target_pairs={{0,1},{1,2},{2,3},{3,0},{4,5},{5,6},{6,7},{7,4},{8,11},{9,8},{10,9... | collective-permute-start | bytes 1769480 | tf_op jit(solution)/shard_map/x/ppermute | solution.py:55
  32.6 4.1 %collective-permute-start.7 = (bf16[256,1152]{1,0:T(8,128)(2,1)S(1)}, bf16[256,1152]{1,0:T(8,128)(2,1)S(1)}, u32[]{:S(2)}, u32[]{:S(2)}) collective-permute-start(bf16[256,1152]{1,0:T(8,128)(2,1)S(1)} %collective-permute-done.5.refs_2_.refs_4_.refs_1_), channel_id=1, source_target_pairs={{0,8},{1,9},{2,10},{3,11},{4,12},{5,13},{6,14},{7,15},{8,0},{9,1},... | collective-permute-start | bytes 1769480 | tf_op jit(solution)/shard_map/core/ppermute | solution.py:55
  39.3 5.4 %collective-permute-start.8 = (bf16[256,1152]{1,0:T(8,128)(2,1)S(1)}, bf16[256,1152]{1,0:T(8,128)(2,1)S(1)}, u32[]{:S(2)}, u32[]{:S(2)}) collective-permute-start(bf16[256,1152]{1,0:T(8,128)(2,1)S(1)} %get-tuple-element.55), channel_id=1, source_target_pairs={{0,8},{1,9},{2,10},{3,11},{4,12},{5,13},{6,14},{7,15},{8,0},{9,1},... | collective-permute-start | bytes 1769480 | tf_op jit(solution)/shard_map/core/ppermute | solution.py:55
  47.0 10.9 %collective-permute-start.11 = (bf16[256,1152]{1,0:T(8,128)(2,1)S(1)}, bf16[256,1152]{1,0:T(8,128)(2,1)S(1)}, u32[]{:S(2)}, u32[]{:S(2)}) collective-permute-start(bf16[256,1152]{1,0:T(8,128)(2,1)S(1)} %get-tuple-element.73), channel_id=1, source_target_pairs={{0,252},{1,253},{2,254},{3,255},{4,248},{5,249},{6,250},{7,251},{8... | collective-permute-start | bytes 1769480 | tf_op jit(solution)/shard_map/q/ppermute | solution.py:55
  47.1 13.4 %collective-permute-start.10 = (bf16[272,1152]{1,0:T(8,128)(2,1)S(1)}, bf16[272,1152]{1,0:T(8,128)(2,1)S(1)}, u32[]{:S(2)}, u32[]{:S(2)}) collective-permute-start(bf16[272,1152]{1,0:T(8,128)(2,1)S(1)} %get-tuple-element.72), channel_id=1, source_target_pairs={{0,1},{1,2},{2,3},{3,0},{4,5},{5,6},{6,7},{7,4},{8,11},{9,8},{10,9... | collective-permute-start | bytes 1880072 | tf_op jit(solution)/shard_map/x/ppermute | solution.py:55
  47.3 15.0 %collective-permute-start.9 = (bf16[272,1152]{1,0:T(8,128)(2,1)S(1)}, bf16[272,1152]{1,0:T(8,128)(2,1)S(1)}, u32[]{:S(2)}, u32[]{:S(2)}) collective-permute-start(bf16[272,1152]{1,0:T(8,128)(2,1)S(1)} %get-tuple-element.63), channel_id=1, source_target_pairs={{0,3},{1,0},{2,1},{3,2},{4,7},{5,4},{6,5},{7,6},{8,9},{9,10},{10,1... | collective-permute-start | bytes 1880072 | tf_op jit(solution)/shard_map/x/ppermute | solution.py:55
  51.2 17.8 %collective-permute-start.13 = (bf16[256,1152]{1,0:T(8,128)(2,1)S(1)}, bf16[256,1152]{1,0:T(8,128)(2,1)S(1)}, u32[]{:S(2)}, u32[]{:S(2)}) collective-permute-start(bf16[256,1152]{1,0:T(8,128)(2,1)S(1)} %get-tuple-element.77), channel_id=1, source_target_pairs={{0,8},{1,9},{2,10},{3,11},{4,12},{5,13},{6,14},{7,15},{8,0},{9,1},... | collective-permute-start | bytes 1769480 | tf_op jit(solution)/shard_map/core/ppermute | solution.py:55
  54.9 14.1 %collective-permute-start.14 = (bf16[256,1152]{1,0:T(8,128)(2,1)S(1)}, bf16[256,1152]{1,0:T(8,128)(2,1)S(1)}, u32[]{:S(2)}, u32[]{:S(2)}) collective-permute-start(bf16[256,1152]{1,0:T(8,128)(2,1)S(1)} %get-tuple-element.79), channel_id=1, source_target_pairs={{0,248},{1,249},{2,250},{3,251},{4,252},{5,253},{6,254},{7,255},{8... | collective-permute-start | bytes 1769480 | tf_op jit(solution)/shard_map/q/ppermute | solution.py:55
  58.1 15.4 %collective-permute-start.15 = (bf16[256,1152]{1,0:T(8,128)(2,1)S(1)}, bf16[256,1152]{1,0:T(8,128)(2,1)S(1)}, u32[]{:S(2)}, u32[]{:S(2)}) collective-permute-start(bf16[256,1152]{1,0:T(8,128)(2,1)S(1)} %joined.3), channel_id=1, source_target_pairs={{0,252},{1,253},{2,254},{3,255},{4,248},{5,249},{6,250},{7,251},{8... | collective-permute-start | bytes 1769480 | tf_op jit(solution)/shard_map/q/ppermute | solution.py:55
  62.4 12.2 %collective-permute-start.12 = (bf16[272,1152]{1,0:T(8,128)(2,1)S(1)}, bf16[272,1152]{1,0:T(8,128)(2,1)S(1)}, u32[]{:S(2)}, u32[]{:S(2)}) collective-permute-start(bf16[272,1152]{1,0:T(8,128)(2,1)S(1)} %joined.2), channel_id=1, source_target_pairs={{0,1},{1,2},{2,3},{3,0},{4,5},{5,6},{6,7},{7,4},{8,11},{9,8},{10,9... | collective-permute-start | bytes 1880072 | tf_op jit(solution)/shard_map/x/ppermute | solution.py:55

commit v4 on v3

--- a/solution.py
+++ b/solution.py
@@ -319,7 +319,7 @@
     )
     from_core = across(g["c0"])
     from_next = qs(tied(g["t1"], g["c0"]), -1)
-    text_prev = qs(joined(g["t2"], text_far), 1)
+    text_prev = qs(joined(g["t2"], tied(text_far, image_far)), 1)
     image_prev = xs(joined(g["i2"], tied(image_far, text_far, image_next)), 1)
     row_loss = loss[0]
     for s in (image_next, image_prev):

time: 76.4 us -> 75.3 us (0.986)
  waiting for transfers between devices: 25.3 us -> 23.8 us
    ppermute x16, waiting for transfers between devices: 25.3 us -> 23.8 us  [moved(): return lax.ppermute(value, AXES, pairs)]
  transfers between devices with their start and end apart: 16 -> 16, of which waited for: 8 -> 7; matrix products, arithmetic and copies ran while one was open for 2% -> 2% of each run, Pallas kernels for 23% -> 26%
where the time goes in v4:
time: 75.3 us; the launch traced here: 75 us
  waiting for transfers between devices  23.8 us (32%)
  Pallas kernels  22.2 us (29%)
  starting transfers between devices  21.4 us (28%)
  other arithmetic  2.88 us (4%)
  local copies, waits for them, and re-layouts  2.83 us (4%)
  between operations  2.04 us (3%)
    ppermute x16, waiting for transfers between devices, moved(): return lax.ppermute(value, AXES, pairs)  23.8 us
    pallas_call x7, Pallas kernels, pair_call(): pl.pallas_call(functools.partial(pairs_kernel, plan), name=name, out_shap...  21.9 us
    ppermute x16, starting transfers between devices, moved(): return lax.ppermute(value, AXES, pairs)  21.4 us
    unnamed x6, local copies, waits for them, and re-layouts  2.83 us
    convert_element_type x2, other arithmetic, summed(): return total.astype(BF16)  2.16 us
  transfers between devices with their start and end apart: 16, of which 7 were waited for; matrix products, arithmetic and copies ran while one was open for 2% of the time, Pallas kernels for 26%

profile of v4, /device:TPU:1, one launch (start us, length us, event | category | flops | bytes accessed | tf_op | source)
XLA Modules:
  0.0 75.0 jit_solution(12987223622454990741)
XLA Ops:
  0.6 3.3 %collective-permute-start = (bf16[256,1152]{1,0:T(8,128)(2,1)}, bf16[256,1152]{1,0:T(8,128)(2,1)S(1)}, u32[]{:S(2)}, u32[]{:S(2)}) collective-permute-start(bf16[256,1152]{1,0:T(8,128)(2,1)} %refs_1_.1), channel_id=1, source_target_pairs={{0,8},{1,9},{2,10},{3,11},{4,12},{5,13},{6,14},{7,15},{8,0},{9,1},... | collective-permute-start | bytes 1769480 | tf_op jit(solution)/shard_map/core/ppermute | solution.py:55
  4.0 0.0 collective-permute-start.4
  4.0 2.0 %collective-permute-start.1 = (bf16[256,1152]{1,0:T(8,128)(2,1)}, bf16[256,1152]{1,0:T(8,128)(2,1)S(1)}, u32[]{:S(2)}, u32[]{:S(2)}) collective-permute-start(bf16[256,1152]{1,0:T(8,128)(2,1)} %refs_0_.1), channel_id=1, source_target_pairs={{0,1},{1,2},{2,3},{3,0},{4,5},{5,6},{6,7},{7,4},{8,11},{9,8},{10,9... | collective-permute-start | bytes 1769480 | tf_op jit(solution)/shard_map/x/ppermute | solution.py:55
  6.0 0.0 collective-permute-start.2
  6.0 4.2 %collective-permute-start.6 = (bf16[256,1152]{1,0:T(8,128)(2,1)}, bf16[256,1152]{1,0:T(8,128)(2,1)S(1)}, u32[]{:S(2)}, u32[]{:S(2)}) collective-permute-start(bf16[256,1152]{1,0:T(8,128)(2,1)} %refs_1_.1), channel_id=1, source_target_pairs={{0,248},{1,249},{2,250},{3,251},{4,252},{5,253},{6,254},{7,255},{8... | collective-permute-start | bytes 1769480 | tf_op jit(solution)/shard_map/q/ppermute | solution.py:55
  11.4 0.1 pad_add_fusion.at_ref
  11.5 0.1 pad_maximum_fusion.factors_ref
  11.6 0.0 collective-permute-done.refs_2_.refs_6_.refs_4_
  11.6 1.1 %copy-done = bf16[256,1152]{1,0:T(8,128)(2,1)S(1)} copy-done((bf16[256,1152]{1,0:T(8,128)(2,1)S(1)}, bf16[256,1152]{1,0:T(8,128)(2,1)}, u32[]{:S(2)}) %copy-start) | copy-done | bytes 589848
  12.7 1.1 %copy-done.1 = bf16[256,1152]{1,0:T(8,128)(2,1)S(1)} copy-done((bf16[256,1152]{1,0:T(8,128)(2,1)S(1)}, bf16[256,1152]{1,0:T(8,128)(2,1)}, u32[]{:S(2)}) %copy-start.1) | copy-done | bytes 589848
  13.7 0.7 copy-done.2
  14.4 2.5 %own.1 = (bf16[256,1152]{1,0:T(8,128)(2,1)S(1)}, bf16[256,1152]{1,0:T(8,128)(2,1)S(1)}, bf16[256,1152]{1,0:T(8,128)(2,1)S(1)}, bf16[256,1152]{1,0:T(8,128)(2,1)S...) custom-call(s32[2]{0:T(128)S(1)} %pad_add_fusion.at_ref, ...), custom_call_target="tpu_custom_call" | custom-call | flops 905969664 | bytes 6488064 | tf_op jit(solution)/shard_map/own/pallas_call | solution.py:192
  16.9 0.0 collective-permute-done.4.refs_4_.refs_2_
  17.0 0.1 collective-permute-start.5
  17.0 0.0 collective-permute-done.1.refs_1_.refs_0_
  17.1 0.3 collective-permute-start.3
  17.3 0.2 collective-permute-done.2.refs_2_
  17.6 5.2 %collective-permute-done.6.refs_5_.refs_3_ = bf16[256,1152]{1,0:T(8,128)(2,1)S(1)} collective-permute-done((bf16[256,1152]{1,0:T(8,128)(2,1)}, bf16[256,1152]{1,0:T(8,128)(2,1)S(1)}, u32[]{:S(2)}, u32[]{:S(2)}) %collective-permute-start.6) | collective-permute-done | bytes 589856 | tf_op jit(solution)/shard_map/q/ppermute | solution.py:55
  22.7 7.2 %near.1 = (bf16[256,1152]{1,0:T(8,128)(2,1)S(1)}, bf16[256,1152]{1,0:T(8,128)(2,1)S(1)}, bf16[256,1152]{1,0:T(8,128)(2,1)S(1)}, bf16[256,1152]{1,0:T(8,128)(2,1)...) custom-call(s32[2]{0:T(128)S(1)} %pad_add_fusion.at_ref, ...), custom_call_target="tpu_custom_call" | custom-call | flops 4529848320 | bytes 11796480 | tf_op jit(solution)/shard_map/near/pallas_call | solution.py:192
  29.9 2.8 %collective-permute-done.5.refs_2_.refs_4_.refs_1_ = bf16[256,1152]{1,0:T(8,128)(2,1)S(1)} collective-permute-done((bf16[256,1152]{1,0:T(8,128)(2,1)S(1)}, bf16[256,1152]{1,0:T(8,128)(2,1)S(1)}, u32[]{:S(2)}, u32[]{:S(2)}) %collective-permute-start.5) | collective-permute-done | bytes 589856 | tf_op jit(solution)/shard_map/q/ppermute | solution.py:55
  32.6 1.3 %collective-permute-start.7 = (bf16[256,1152]{1,0:T(8,128)(2,1)S(1)}, bf16[256,1152]{1,0:T(8,128)(2,1)S(1)}, u32[]{:S(2)}, u32[]{:S(2)}) collective-permute-start(bf16[256,1152]{1,0:T(8,128)(2,1)S(1)} %collective-permute-done.5.refs_2_.refs_4_.refs_1_), channel_id=1, source_target_pairs={{0,8},{1,9},{2,10},{3,11},{4,12},{5,13},{6,14},{7,15},{8,0},{9,1},... | collective-permute-start | bytes 1769480 | tf_op jit(solution)/shard_map/core/ppermute | solution.py:55
  34.0 2.7 %third.1 = (bf16[256,1152]{1,0:T(8,128)(2,1)S(1)}, bf16[256,1152]{1,0:T(8,128)(2,1)S(1)}, f32[8,256]{1,0:T(8,128)S(1)}, bf16[256,1024]{1,0:T(8,128)(2,1)S(1)}) custom-call(s32[2]{0:T(128)S(1)} %pad_add_fusion.at_ref, f32[3]{0:T(128)S(1)} %pad_maximum_fusion.factors_ref, s32[1,2048]{1,0:T(1,128)S(1)} %get-tuple-element.43.slot_ref, ...), custom_call_target="tpu_custom_call" | custom-call | flops 1358954496 | bytes 6488064 | tf_op jit(solution)/shard_map/third/pallas_call | solution.py:192
  36.7 0.0 collective-permute-done.7.refs_4_.refs_3_.refs_2_
  36.7 2.5 %across.1 = (bf16[256,1152]{1,0:T(8,128)(2,1)S(1)}, f32[8,256]{1,0:T(8,128)S(1)}, bf16[1024,256]{1,0:T(8,128)(2,1)S(1)}) custom-call(s32[2]{0:T(128)S(1)} %pad_add_fusion.at_ref, f32[3]{0:T(128)S(1)} %pad_maximum_fusion.factors_ref, s32[1,2048]{1,0:T(1,128)S(1)} %get-tuple-element.43.slot_ref, bf16[256,1152]{1,0:T(8,128)(2,1)S(1)} %get-tuple-element.44.refs_0_, ...), custom_call_target="tpu_custom_call" | custom-call | flops 1207959552 | bytes 5308416 | tf_op jit(solution)/shard_map/across/pallas_call | solution.py:192
  39.2 3.0 %collective-permute-start.8 = (bf16[256,1152]{1,0:T(8,128)(2,1)S(1)}, bf16[256,1152]{1,0:T(8,128)(2,1)S(1)}, u32[]{:S(2)}, u32[]{:S(2)}) collective-permute-start(bf16[256,1152]{1,0:T(8,128)(2,1)S(1)} %get-tuple-element.56), channel_id=1, source_target_pairs={{0,8},{1,9},{2,10},{3,11},{4,12},{5,13},{6,14},{7,15},{8,0},{9,1},... | collective-permute-start | bytes 1769480 | tf_op jit(solution)/shard_map/core/ppermute | solution.py:55
  42.2 2.2 %far.1 = (bf16[272,1152]{1,0:T(8,128)(2,1)S(1)}, bf16[272,1152]{1,0:T(8,128)(2,1)S(1)}, f32[8,256]{1,0:T(8,128)S(1)}, bf16[512,256]{1,0:T(8,128)(2,1)S(1)}) custom-call(s32[2]{0:T(128)S(1)} %pad_add_fusion.at_ref, f32[3]{0:T(128)S(1)} %pad_maximum_fusion.factors_ref, s32[1,2048]{1,0:T(1,128)S(1)} %get-tuple-element.43.slot_ref, ...), custom_call_target="tpu_custom_call" | custom-call | flops 905969664 | bytes 7077888 | tf_op jit(solution)/shard_map/far/pallas_call | solution.py:192
  44.4 0.4 collective-permute-start.10
  44.8 0.0 collective-permute-done.8.refs_5_.refs_8_
  44.8 2.3 %rest.1 = (bf16[256,1152]{1,0:T(8,128)(2,1)S(1)}, f32[8,256]{1,0:T(8,128)S(1)}, bf16[512,256]{1,0:T(8,128)(2,1)S(1)}) custom-call(s32[2]{0:T(128)S(1)} %pad_add_fusion.at_ref, f32[3]{0:T(128)S(1)} %pad_maximum_fusion.factors_ref, s32[1,2048]{1,0:T(1,128)S(1)} %get-tuple-element.43.slot_ref, bf16[256,1152]{1,0:T(8,128)(2,1)S(1)} %get-tuple-element.44.refs_0_, ...), custom_call_target="tpu_custom_call" | custom-call | flops 905969664 | bytes 6488064 | tf_op jit(solution)/shard_map/rest/pallas_call | solution.py:192
  47.1 0.1 collective-permute-start.11
  47.2 1.5 %collective-permute-start.9 = (bf16[272,1152]{1,0:T(8,128)(2,1)S(1)}, bf16[272,1152]{1,0:T(8,128)(2,1)S(1)}, u32[]{:S(2)}, u32[]{:S(2)}) collective-permute-start(bf16[272,1152]{1,0:T(8,128)(2,1)S(1)} %get-tuple-element.64), channel_id=1, source_target_pairs={{0,3},{1,0},{2,1},{3,2},{4,7},{5,4},{6,5},{7,6},{8,9},{9,10},{10,1... | collective-permute-start | bytes 1880072 | tf_op jit(solution)/shard_map/x/ppermute | solution.py:55
  48.7 2.5 %wrap.1 = (bf16[256,1152]{1,0:T(8,128)(2,1)S(1)}, bf16[256,1152]{1,0:T(8,128)(2,1)S(1)}, bf16[256,1152]{1,0:T(8,128)(2,1)S(1)}, bf16[272,1152]{1,0:T(8,128)(2,1)...) custom-call(s32[2]{0:T(128)S(1)} %pad_add_fusion.at_ref, ...), custom_call_target="tpu_custom_call" | custom-call | flops 1056964608 | bytes 11796480 | tf_op jit(solution)/shard_map/wrap/pallas_call | solution.py:192
  51.2 2.6 %collective-permute-start.13 = (bf16[256,1152]{1,0:T(8,128)(2,1)S(1)}, bf16[256,1152]{1,0:T(8,128)(2,1)S(1)}, u32[]{:S(2)}, u32[]{:S(2)}) collective-permute-start(bf16[256,1152]{1,0:T(8,128)(2,1)S(1)} %get-tuple-element.78), channel_id=1, source_target_pairs={{0,8},{1,9},{2,10},{3,11},{4,12},{5,13},{6,14},{7,15},{8,0},{9,1},... | collective-permute-start | bytes 1769480 | tf_op jit(solution)/shard_map/core/ppermute | solution.py:55
  53.8 0.0 collective-permute-start.14
  53.8 0.8 %collective-permute-done.10.right = bf16[272,1152]{1,0:T(8,128)(2,1)S(1)} collective-permute-done((bf16[272,1152]{1,0:T(8,128)(2,1)S(1)}, bf16[272,1152]{1,0:T(8,128)(2,1)S(1)}, u32[]{:S(2)}, u32[]{:S(2)}) %collective-permute-start.10) | collective-permute-done | bytes 626720 | tf_op jit(solution)/shard_map/x/ppermute | solution.py:55
  54.6 5.8 %collective-permute-done.11.right = bf16[256,1152]{1,0:T(8,128)(2,1)S(1)} collective-permute-done((bf16[256,1152]{1,0:T(8,128)(2,1)S(1)}, bf16[256,1152]{1,0:T(8,128)(2,1)S(1)}, u32[]{:S(2)}, u32[]{:S(2)}) %collective-permute-start.11) | collective-permute-done | bytes 589856 | tf_op jit(solution)/shard_map/q/ppermute | solution.py:55
  60.4 0.1 joined.3
  60.5 2.6 %collective-permute-start.15 = (bf16[256,1152]{1,0:T(8,128)(2,1)S(1)}, bf16[256,1152]{1,0:T(8,128)(2,1)S(1)}, u32[]{:S(2)}, u32[]{:S(2)}) collective-permute-start(bf16[256,1152]{1,0:T(8,128)(2,1)S(1)} %joined.3), channel_id=1, source_target_pairs={{0,252},{1,253},{2,254},{3,255},{4,248},{5,249},{6,250},{7,251},{8... | collective-permute-start | bytes 1769480 | tf_op jit(solution)/shard_map/q/ppermute | solution.py:55
  63.1 0.0 collective-permute-done.9
  63.1 0.2 joined.2
  63.2 0.1 collective-permute-start.12
  63.3 3.6 %collective-permute-done.14 = bf16[256,1152]{1,0:T(8,128)(2,1)S(1)} collective-permute-done((bf16[256,1152]{1,0:T(8,128)(2,1)S(1)}, bf16[256,1152]{1,0:T(8,128)(2,1)S(1)}, u32[]{:S(2)}, u32[]{:S(2)}) %collective-permute-start.14) | collective-permute-done | bytes 589856 | tf_op jit(solution)/shard_map/q/ppermute | solution.py:55
  66.9 0.0 collective-permute-done.13
  66.9 5.4 %collective-permute-done.15 = bf16[256,1152]{1,0:T(8,128)(2,1)S(1)} collective-permute-done((bf16[256,1152]{1,0:T(8,128)(2,1)S(1)}, bf16[256,1152]{1,0:T(8,128)(2,1)S(1)}, u32[]{:S(2)}, u32[]{:S(2)}) %collective-permute-start.15) | collective-permute-done | bytes 589856 | tf_op jit(solution)/shard_map/q/ppermute | solution.py:55
  72.3 1.1 %add_convert_fusion = bf16[256,1152]{1,0:T(8,128)(2,1)} fusion(bf16[256,1152]{1,0:T(8,128)(2,1)S(1)} %collective-permute-done.15, bf16[256,1152]{1,0:T(8,128)(2,1)S(1)} %collective-permute-done.14, bf16[256,1152]{1,0:T(8,128)(2,1)S(1)} %collective-permute-done.13, bf16[256,1152]{1,0:T(8,128)(2,1)S(1)} %get-tuple-element.77), kind=kLoop, calls=%fused_computation | loop fusion | flops 2359296 | bytes 2949120 | tf_op jit(solution)/shard_map/convert_element_type | solution.py:243
  73.4 0.0 collective-permute-done.12
  73.4 0.6 fusion.1
  74.0 1.0 %add_convert_fusion.1 = bf16[256,1152]{1,0:T(8,128)(2,1)} fusion(bf16[256,1152]{1,0:T(8,128)(2,1)S(1)} %get-tuple-element.76, bf16[272,1152]{1,0:T(8,128)(2,1)S(1)} %collective-permute-done.12, bf16[272,1152]{1,0:T(8,128)(2,1)S(1)} %collective-permute-done.9), kind=kLoop, calls=%fused_computation.1 | loop fusion | flops 1769472 | bytes 2359296 | tf_op jit(solution)/shard_map/convert_element_type | solution.py:243
  (4 shorter events, 0.0 us)
Async XLA Ops:
  0.6 11.0 %collective-permute-start = (bf16[256,1152]{1,0:T(8,128)(2,1)}, bf16[256,1152]{1,0:T(8,128)(2,1)S(1)}, u32[]{:S(2)}, u32[]{:S(2)}) collective-permute-start(bf16[256,1152]{1,0:T(8,128)(2,1)} %refs_1_.1), channel_id=1, source_target_pairs={{0,8},{1,9},{2,10},{3,11},{4,12},{5,13},{6,14},{7,15},{8,0},{9,1},... | collective-permute-start | bytes 1769480 | tf_op jit(solution)/shard_map/core/ppermute | solution.py:55
  4.0 13.0 %collective-permute-start.4 = (bf16[256,1152]{1,0:T(8,128)(2,1)}, bf16[256,1152]{1,0:T(8,128)(2,1)S(1)}, u32[]{:S(2)}, u32[]{:S(2)}) collective-permute-start(bf16[256,1152]{1,0:T(8,128)(2,1)} %refs_1_.1), channel_id=1, source_target_pairs={{0,252},{1,253},{2,254},{3,255},{4,248},{5,249},{6,250},{7,251},{8... | collective-permute-start | bytes 1769480 | tf_op jit(solution)/shard_map/q/ppermute | solution.py:55
  4.0 13.1 %collective-permute-start.1 = (bf16[256,1152]{1,0:T(8,128)(2,1)}, bf16[256,1152]{1,0:T(8,128)(2,1)S(1)}, u32[]{:S(2)}, u32[]{:S(2)}) collective-permute-start(bf16[256,1152]{1,0:T(8,128)(2,1)} %refs_0_.1), channel_id=1, source_target_pairs={{0,1},{1,2},{2,3},{3,0},{4,5},{5,6},{6,7},{7,4},{8,11},{9,8},{10,9... | collective-permute-start | bytes 1769480 | tf_op jit(solution)/shard_map/x/ppermute | solution.py:55
  6.0 11.6 %collective-permute-start.2 = (bf16[256,1152]{1,0:T(8,128)(2,1)}, bf16[256,1152]{1,0:T(8,128)(2,1)S(1)}, u32[]{:S(2)}, u32[]{:S(2)}) collective-permute-start(bf16[256,1152]{1,0:T(8,128)(2,1)} %refs_0_.1), channel_id=1, source_target_pairs={{0,3},{1,0},{2,1},{3,2},{4,7},{5,4},{6,5},{7,6},{8,9},{9,10},{10,1... | collective-permute-start | bytes 1769480 | tf_op jit(solution)/shard_map/x/ppermute | solution.py:55
  6.0 16.7 %collective-permute-start.6 = (bf16[256,1152]{1,0:T(8,128)(2,1)}, bf16[256,1152]{1,0:T(8,128)(2,1)S(1)}, u32[]{:S(2)}, u32[]{:S(2)}) collective-permute-start(bf16[256,1152]{1,0:T(8,128)(2,1)} %refs_1_.1), channel_id=1, source_target_pairs={{0,248},{1,249},{2,250},{3,251},{4,252},{5,253},{6,254},{7,255},{8... | collective-permute-start | bytes 1769480 | tf_op jit(solution)/shard_map/q/ppermute | solution.py:55
  11.6 1.1 %copy-start = (bf16[256,1152]{1,0:T(8,128)(2,1)S(1)}, bf16[256,1152]{1,0:T(8,128)(2,1)}, u32[]{:S(2)}) copy-start(bf16[256,1152]{1,0:T(8,128)(2,1)} %refs_0_.1) | copy-start | bytes 1769476
  12.7 1.1 %copy-start.1 = (bf16[256,1152]{1,0:T(8,128)(2,1)S(1)}, bf16[256,1152]{1,0:T(8,128)(2,1)}, u32[]{:S(2)}) copy-start(bf16[256,1152]{1,0:T(8,128)(2,1)} %refs_1_.1) | copy-start | bytes 1769476
  13.7 0.7 copy-start.2
  17.0 15.7 %collective-permute-start.5 = (bf16[256,1152]{1,0:T(8,128)(2,1)S(1)}, bf16[256,1152]{1,0:T(8,128)(2,1)S(1)}, u32[]{:S(2)}, u32[]{:S(2)}) collective-permute-start(bf16[256,1152]{1,0:T(8,128)(2,1)S(1)} %collective-permute-done.4.refs_4_.refs_2_), channel_id=1, source_target_pairs={{0,252},{1,253},{2,254},{3,255},{4,248},{5,249},{6,250},{7,251},{8... | collective-permute-start | bytes 1769480 | tf_op jit(solution)/shard_map/q/ppermute | solution.py:55
  17.1 16.9 %collective-permute-start.3 = (bf16[256,1152]{1,0:T(8,128)(2,1)S(1)}, bf16[256,1152]{1,0:T(8,128)(2,1)S(1)}, u32[]{:S(2)}, u32[]{:S(2)}) collective-permute-start(bf16[256,1152]{1,0:T(8,128)(2,1)S(1)} %collective-permute-done.1.refs_1_.refs_0_), channel_id=1, source_target_pairs={{0,1},{1,2},{2,3},{3,0},{4,5},{5,6},{6,7},{7,4},{8,11},{9,8},{10,9... | collective-permute-start | bytes 1769480 | tf_op jit(solution)/shard_map/x/ppermute | solution.py:55
  32.6 4.0 %collective-permute-start.7 = (bf16[256,1152]{1,0:T(8,128)(2,1)S(1)}, bf16[256,1152]{1,0:T(8,128)(2,1)S(1)}, u32[]{:S(2)}, u32[]{:S(2)}) collective-permute-start(bf16[256,1152]{1,0:T(8,128)(2,1)S(1)} %collective-permute-done.5.refs_2_.refs_4_.refs_1_), channel_id=1, source_target_pairs={{0,8},{1,9},{2,10},{3,11},{4,12},{5,13},{6,14},{7,15},{8,0},{9,1},... | collective-permute-start | bytes 1769480 | tf_op jit(solution)/shard_map/core/ppermute | solution.py:55
  39.2 5.6 %collective-permute-start.8 = (bf16[256,1152]{1,0:T(8,128)(2,1)S(1)}, bf16[256,1152]{1,0:T(8,128)(2,1)S(1)}, u32[]{:S(2)}, u32[]{:S(2)}) collective-permute-start(bf16[256,1152]{1,0:T(8,128)(2,1)S(1)} %get-tuple-element.56), channel_id=1, source_target_pairs={{0,8},{1,9},{2,10},{3,11},{4,12},{5,13},{6,14},{7,15},{8,0},{9,1},... | collective-permute-start | bytes 1769480 | tf_op jit(solution)/shard_map/core/ppermute | solution.py:55
  44.4 10.2 %collective-permute-start.10 = (bf16[272,1152]{1,0:T(8,128)(2,1)S(1)}, bf16[272,1152]{1,0:T(8,128)(2,1)S(1)}, u32[]{:S(2)}, u32[]{:S(2)}) collective-permute-start(bf16[272,1152]{1,0:T(8,128)(2,1)S(1)} %get-tuple-element.73), channel_id=1, source_target_pairs={{0,1},{1,2},{2,3},{3,0},{4,5},{5,6},{6,7},{7,4},{8,11},{9,8},{10,9... | collective-permute-start | bytes 1880072 | tf_op jit(solution)/shard_map/x/ppermute | solution.py:55
  47.1 13.2 %collective-permute-start.11 = (bf16[256,1152]{1,0:T(8,128)(2,1)S(1)}, bf16[256,1152]{1,0:T(8,128)(2,1)S(1)}, u32[]{:S(2)}, u32[]{:S(2)}) collective-permute-start(bf16[256,1152]{1,0:T(8,128)(2,1)S(1)} %get-tuple-element.74), channel_id=1, source_target_pairs={{0,252},{1,253},{2,254},{3,255},{4,248},{5,249},{6,250},{7,251},{8... | collective-permute-start | bytes 1769480 | tf_op jit(solution)/shard_map/q/ppermute | solution.py:55
  47.2 15.8 %collective-permute-start.9 = (bf16[272,1152]{1,0:T(8,128)(2,1)S(1)}, bf16[272,1152]{1,0:T(8,128)(2,1)S(1)}, u32[]{:S(2)}, u32[]{:S(2)}) collective-permute-start(bf16[272,1152]{1,0:T(8,128)(2,1)S(1)} %get-tuple-element.64), channel_id=1, source_target_pairs={{0,3},{1,0},{2,1},{3,2},{4,7},{5,4},{6,5},{7,6},{8,9},{9,10},{10,1... | collective-permute-start | bytes 1880072 | tf_op jit(solution)/shard_map/x/ppermute | solution.py:55
  51.2 15.7 %collective-permute-start.13 = (bf16[256,1152]{1,0:T(8,128)(2,1)S(1)}, bf16[256,1152]{1,0:T(8,128)(2,1)S(1)}, u32[]{:S(2)}, u32[]{:S(2)}) collective-permute-start(bf16[256,1152]{1,0:T(8,128)(2,1)S(1)} %get-tuple-element.78), channel_id=1, source_target_pairs={{0,8},{1,9},{2,10},{3,11},{4,12},{5,13},{6,14},{7,15},{8,0},{9,1},... | collective-permute-start | bytes 1769480 | tf_op jit(solution)/shard_map/core/ppermute | solution.py:55
  53.8 13.2 %collective-permute-start.14 = (bf16[256,1152]{1,0:T(8,128)(2,1)S(1)}, bf16[256,1152]{1,0:T(8,128)(2,1)S(1)}, u32[]{:S(2)}, u32[]{:S(2)}) collective-permute-start(bf16[256,1152]{1,0:T(8,128)(2,1)S(1)} %get-tuple-element.80), channel_id=1, source_target_pairs={{0,248},{1,249},{2,250},{3,251},{4,252},{5,253},{6,254},{7,255},{8... | collective-permute-start | bytes 1769480 | tf_op jit(solution)/shard_map/q/ppermute | solution.py:55
  60.5 11.8 %collective-permute-start.15 = (bf16[256,1152]{1,0:T(8,128)(2,1)S(1)}, bf16[256,1152]{1,0:T(8,128)(2,1)S(1)}, u32[]{:S(2)}, u32[]{:S(2)}) collective-permute-start(bf16[256,1152]{1,0:T(8,128)(2,1)S(1)} %joined.3), channel_id=1, source_target_pairs={{0,252},{1,253},{2,254},{3,255},{4,248},{5,249},{6,250},{7,251},{8... | collective-permute-start | bytes 1769480 | tf_op jit(solution)/shard_map/q/ppermute | solution.py:55
  63.2 10.2 %collective-permute-start.12 = (bf16[272,1152]{1,0:T(8,128)(2,1)S(1)}, bf16[272,1152]{1,0:T(8,128)(2,1)S(1)}, u32[]{:S(2)}, u32[]{:S(2)}) collective-permute-start(bf16[272,1152]{1,0:T(8,128)(2,1)S(1)} %joined.2), channel_id=1, source_target_pairs={{0,1},{1,2},{2,3},{3,0},{4,5},{5,6},{6,7},{7,4},{8,11},{9,8},{10,9... | collective-permute-start | bytes 1880072 | tf_op jit(solution)/shard_map/x/ppermute | solution.py:55
